TPU v7x, 32 devices: a whole 2x2x4 slice. The times are simulated.
32 devices in a mesh: tx: 4 (over z), ty: 8 (over y, x, core).
Axes of the slice: x: 2, y: 2, z: 4, core: 2. Of those that a mesh axis runs over, the one named last changes fastest.
Arguments:
- hidden_in: bfloat16 [128, 8192], P(None, ('ty', 'tx'))
- norm_gain: bfloat16 [8192], P(('ty', 'tx')), may hold values from 0.5 to 1.5
- qkv_weight: bfloat16 [8192, 10240], P('ty', 'tx'), may hold values from -0.0625 to 0.0625
- qkv_bias: bfloat16 [10240], replicated, may hold values from -4 to 4
- key_cache: bfloat16 [128, 128, 1024], P(('ty', 'tx')), may hold values from -6 to 6
- value_cache: bfloat16 [128, 128, 1024], P(('ty', 'tx')), may hold values from -6 to 6
- lengths: int32 [128], P(('ty', 'tx')), may hold values from 1 to 128
- out_weight: bfloat16 [8192, 8192], P('tx', 'ty'), may hold values from -0.0625 to 0.0625
- final_gain: bfloat16 [8192], P(('ty', 'tx')), may hold values from 0.5 to 1.5
- in_weight: bfloat16 [8192, 2048], P('ty', 'tx'), may hold values from -0.0625 to 0.0625
- owners: int32 [128], replicated, may hold values from 0 to 7, as said below
- codebook_ids: int32 [128, 8], replicated, may hold values from 0 to 1023
- mlp_gate: bfloat16 [2048, 4096], P(None, 'tx'), may hold values from -0.125 to 0.125
- mlp_up: bfloat16 [2048, 4096], P(None, 'tx'), may hold values from -0.125 to 0.125
- mlp_down: bfloat16 [4096, 2048], P('tx'), may hold values from -0.09375 to 0.09375
- pre_gain: bfloat16 [2048], replicated, may hold values from 0.5 to 1.5
- head_gain: bfloat16 [2048], replicated, may hold values from 0.5 to 1.5
- codebook_table: bfloat16 [8, 1024, 2048], P(None, 'tx'), may hold values from -0.375 to 0.375
Outputs:
- hidden_out: bfloat16 [128, 8192], P(None, ('ty', 'tx'))
- depth_logprob: float32 [8, 8, 32], P('ty')
Inputs may be any that keep to these rules, and one draw needn't show every extreme that they name: `owners`: in each of the 8 aligned blocks of 16 rows no owner is named more than 4 times, and one owner is named exactly 4 times in every block.
All inputs are finite; a program needn't handle non-finite values.
Results may differ from a plain program's by a relative error of at most 0.0095.
Values may be sent and summed in bfloat16 or wider, within the bound.
A program may use at most 128 MiB of HBM per device.

v0:
```python
import jax
import jax.numpy as jnp
from jax import lax
from jax.sharding import PartitionSpec as P

HEADS = 64
KV_HEADS = 8
HEAD_DIM = 128
STEPS = 8
LMAX = 128


epsilon = 1e-06
rope_base = 1000000.0
embed_gain = 16.0


def rms_scale(values, gain):
    mean_square = jnp.mean(values * values, axis=-1, keepdims=True)
    return values * lax.rsqrt(mean_square + epsilon) * gain.astype(jnp.float32)


def rotate(values, position):
    half_dim = values.shape[-1] // 2
    frequency = jnp.exp(
        -jnp.log(rope_base) * (2.0 * jnp.arange(half_dim, dtype=jnp.float32) / values.shape[-1])
    )
    phase_angle = position.astype(jnp.float32)[:, None, None] * frequency[None, None, :]
    cosine = jnp.cos(phase_angle)
    sine_part = jnp.sin(phase_angle)
    first_half = values[..., :half_dim]
    second_half = values[..., half_dim:]
    return jnp.concatenate(
        [
            first_half * cosine - second_half * sine_part,
            second_half * cosine + first_half * sine_part,
        ],
        axis=-1,
    )


def attend(query_heads, new_key, new_value, key_cache, value_cache, lengths):
    row_count = query_heads.shape[0]
    group_size = HEADS // KV_HEADS
    query_heads = query_heads.reshape(row_count, KV_HEADS, group_size, HEAD_DIM)
    keys_all = key_cache.reshape(row_count, LMAX, KV_HEADS, HEAD_DIM)
    values_all = value_cache.reshape(row_count, LMAX, KV_HEADS, HEAD_DIM)
    scores = jnp.einsum(
        "rgjd,rtgd->rgjt", query_heads, keys_all, preferred_element_type=jnp.float32
    )
    own_score = jnp.einsum(
        "rgjd,rgd->rgj", query_heads, new_key, preferred_element_type=jnp.float32
    )
    in_cache = jnp.arange(LMAX, dtype=jnp.int32)[None, :] < lengths[:, None]
    weights = jnp.where(in_cache[:, None, None, :], jnp.exp(scores), 0.0)
    own_weight = jnp.exp(own_score)
    denominator = jnp.sum(weights, axis=-1) + own_weight
    probability = (weights / denominator[..., None]).astype(jnp.bfloat16)
    own_prob = (own_weight / denominator).astype(jnp.bfloat16)
    blended = jnp.einsum(
        "rgjt,rtgd->rgjd", probability, values_all, preferred_element_type=jnp.float32
    )
    blended = (
        blended
        + own_prob.astype(jnp.float32)[..., None] * new_value.astype(jnp.float32)[:, :, None, :]
    )
    return blended.reshape(row_count, HEADS * HEAD_DIM).astype(jnp.bfloat16)


def project_with(weight, piece_rows):
    return jnp.dot(piece_rows, weight, preferred_element_type=jnp.float32)


def depth_rows(
    start_rows, slot_codes, mlp_gate, mlp_up, mlp_down, pre_gain, head_gain, codebook_table
):
    depth_state = start_rows.astype(jnp.float32)
    local_entries = codebook_table.shape[1]
    offset = lax.axis_index("tx") * local_entries
    entry_ids = jnp.arange(local_entries, dtype=jnp.int32)
    columns = []
    for step_index in range(STEPS):
        inner_rows = rms_scale(depth_state, pre_gain).astype(jnp.bfloat16)
        gate_part = jnp.dot(inner_rows, mlp_gate, preferred_element_type=jnp.float32)
        up_part = jnp.dot(inner_rows, mlp_up, preferred_element_type=jnp.float32)
        activation = (jax.nn.silu(gate_part) * up_part).astype(jnp.bfloat16)
        down_part = jnp.dot(activation, mlp_down, preferred_element_type=jnp.float32)
        depth_state = depth_state + lax.psum(down_part.astype(jnp.bfloat16), "tx").astype(
            jnp.float32
        )
        outer_rows = rms_scale(depth_state, head_gain).astype(jnp.bfloat16)
        table_rows = codebook_table[step_index]
        logits = lax.dot_general(
            outer_rows, table_rows, (((1,), (1,)), ((), ())), preferred_element_type=jnp.float32
        )
        chosen = slot_codes[:, step_index : step_index + 1] - offset == entry_ids[None, :]
        picked = jnp.sum(jnp.where(chosen, logits, 0.0), axis=1)
        exp_total = jnp.sum(jnp.exp(logits), axis=1)
        if step_index + 1 < STEPS:
            lookup = jnp.dot(
                chosen.astype(jnp.bfloat16), table_rows, preferred_element_type=jnp.float32
            )
            exp_total, picked, lookup = (
                lax.psum(exp_total.astype(jnp.bfloat16), "tx").astype(jnp.float32),
                lax.psum(picked.astype(jnp.bfloat16), "tx").astype(jnp.float32),
                lax.psum(lookup.astype(jnp.bfloat16), "tx").astype(jnp.float32),
            )
            depth_state = depth_state + embed_gain * lookup
        else:
            exp_total, picked = lax.psum((exp_total, picked), "tx")
        columns.append(picked - jnp.log(exp_total))
    return jnp.stack(columns, axis=1)


def body(
    hidden_in,
    norm_gain,
    qkv_weight,
    qkv_bias,
    key_cache,
    value_cache,
    lengths,
    out_weight,
    final_gain,
    in_weight,
    owners,
    codebook_ids,
    mlp_gate,
    mlp_up,
    mlp_down,
    pre_gain,
    head_gain,
    codebook_table,
):
    count_tx = lax.axis_size("tx")
    count_ty = lax.axis_size("ty")
    batch_rows = hidden_in.shape[0]
    own_rows = key_cache.shape[0]
    full_width = hidden_in.shape[1] * count_tx * count_ty
    residual = hidden_in.astype(jnp.float32)
    square_sum = lax.psum(jnp.sum(residual * residual, axis=1), ("tx", "ty"))
    normed = (
        residual
        * lax.rsqrt(square_sum / full_width + epsilon)[:, None]
        * norm_gain.astype(jnp.float32)
    ).astype(jnp.bfloat16)
    partial_qkv = project_with(qkv_weight, lax.all_gather(normed, "tx", axis=1, tiled=True))
    summed = lax.psum_scatter(partial_qkv, "ty", scatter_dimension=1, tiled=True).astype(
        jnp.bfloat16
    )
    piece_width = summed.shape[1]
    ordered = (
        summed.reshape(count_ty, count_tx, own_rows, piece_width)
        .transpose(1, 0, 2, 3)
        .reshape(batch_rows, piece_width)
    )
    qkv_raw = lax.all_to_all(ordered, ("tx", "ty"), split_axis=0, concat_axis=1, tiled=True)
    qkv = qkv_raw.astype(jnp.float32) + qkv_bias.astype(jnp.float32)
    query_width = HEADS * HEAD_DIM
    key_width = KV_HEADS * HEAD_DIM
    query_heads = rotate(qkv[:, :query_width].reshape(own_rows, HEADS, HEAD_DIM), lengths)
    query_heads = (query_heads * HEAD_DIM ** (-0.5)).astype(jnp.bfloat16)
    new_key = rotate(
        qkv[:, query_width : query_width + key_width].reshape(own_rows, KV_HEADS, HEAD_DIM), lengths
    ).astype(jnp.bfloat16)
    new_value = (
        qkv[:, query_width + key_width :].reshape(own_rows, KV_HEADS, HEAD_DIM).astype(jnp.bfloat16)
    )
    attended = attend(query_heads, new_key, new_value, key_cache, value_cache, lengths)
    spread = lax.all_to_all(attended, ("tx", "ty"), split_axis=1, concat_axis=0, tiled=True)
    spread_width = spread.shape[1]
    spread = (
        spread.reshape(count_tx, count_ty, own_rows, spread_width)
        .transpose(1, 0, 2, 3)
        .reshape(batch_rows, spread_width)
    )
    partial_out = project_with(out_weight, lax.all_gather(spread, "ty", axis=1, tiled=True))
    projected = lax.psum_scatter(partial_out, "tx", scatter_dimension=1, tiled=True)
    hidden_out = (residual + projected).astype(jnp.bfloat16)
    leaving = hidden_out.astype(jnp.float32)
    final_sum = lax.psum(jnp.sum(leaving * leaving, axis=1), ("tx", "ty"))
    final_rows = (
        leaving
        * lax.rsqrt(final_sum / full_width + epsilon)[:, None]
        * final_gain.astype(jnp.float32)
    ).astype(jnp.bfloat16)
    partial_start = project_with(in_weight, lax.all_gather(final_rows, "tx", axis=1, tiled=True))
    start_part = lax.psum_scatter(
        partial_start.astype(jnp.bfloat16), "ty", scatter_dimension=0, tiled=True
    )
    depth_start = lax.all_gather(start_part, "tx", axis=1, tiled=True)
    block_rows = depth_start.shape[0]
    capacity = max(2, 2 * own_rows * count_tx // count_ty)
    slot_count = count_ty * capacity
    my_block = lax.axis_index("ty")
    block_owners = lax.dynamic_slice_in_dim(owners, my_block * block_rows, block_rows, 0)
    owner_member = (block_owners[:, None] == jnp.arange(count_ty, dtype=jnp.int32)[None, :]).astype(
        jnp.int32
    )
    send_rank = jnp.sum((jnp.cumsum(owner_member, axis=0) - owner_member) * owner_member, axis=1)
    send_slot = block_owners * capacity + send_rank
    send_select = send_slot[:, None] == jnp.arange(slot_count, dtype=jnp.int32)[None, :]
    outgoing = jnp.dot(
        send_select.T.astype(jnp.bfloat16), depth_start, preferred_element_type=jnp.float32
    ).astype(jnp.bfloat16)
    incoming = lax.all_to_all(
        outgoing.reshape(count_ty, capacity, depth_start.shape[1]),
        "ty",
        split_axis=0,
        concat_axis=0,
        tiled=True,
    )
    arrived = incoming.reshape(slot_count, depth_start.shape[1])
    mine_mask = (owners == my_block).reshape(count_ty, block_rows)
    mine_count = mine_mask.astype(jnp.int32)
    recv_slot = (
        jnp.arange(count_ty, dtype=jnp.int32)[:, None] * capacity
        + jnp.cumsum(mine_count, axis=1)
        - mine_count
    )
    recv_select = (
        (mine_mask[..., None] & (recv_slot[..., None] == jnp.arange(slot_count, dtype=jnp.int32)))
        .reshape(batch_rows, slot_count)
        .astype(jnp.int32)
    )
    slot_codes = jnp.dot(recv_select.T, codebook_ids)
    filled = jnp.sum(recv_select, axis=0)
    slot_codes = jnp.where(filled[:, None] > 0, slot_codes, -1)
    logprob = depth_rows(
        arrived, slot_codes, mlp_gate, mlp_up, mlp_down, pre_gain, head_gain, codebook_table
    )
    logprob = jnp.where(filled[:, None] > 0, logprob, 0.0)
    depth_logprob = logprob.T[None]
    return (hidden_out, depth_logprob)


def solution(mesh):
    placed = (
        P(None, ("ty", "tx")),
        P(("ty", "tx")),
        P("ty", "tx"),
        P(),
        P(("ty", "tx"), None, None),
        P(("ty", "tx"), None, None),
        P(("ty", "tx")),
        P("tx", "ty"),
        P(("ty", "tx")),
        P("ty", "tx"),
        P(),
        P(),
        P(None, "tx"),
        P(None, "tx"),
        P("tx", None),
        P(),
        P(),
        P(None, "tx", None),
    )
    return jax.shard_map(
        body,
        mesh=mesh,
        in_specs=placed,
        out_specs=(P(None, ("ty", "tx")), P("ty", None, None)),
        check_vma=False,
    )
```

profile of v0, /device:TPU:0, one launch (start us, length us, event | category | flops | bytes accessed | tf_op | source)
XLA Modules:
  0.0 665.9 jit_solution(15795414989813338270)
XLA Ops:
  8.9 42.0 %psum.231 = f32[128]{0:T(128)S(1)} all-reduce(f32[128]{0:T(128)S(1)} %fusion.55), channel_id=1, replica_groups=mesh['tx'=4,'ty'=8] {'tx','ty'}, use_global_device_ids=true, to_apply=%region_1.0 | all-reduce | flops 128 | bytes 1024 | tf_op jit(solution)/shard_map/psum | solution.py:141
  51.9 14.5 %all_gather.12 = bf16[128,1024]{1,0:T(8,128)(2,1)S(1)} all-gather(bf16[128,256]{1,0:T(8,128)(2,1)S(1)} %fusion.57), channel_id=1, replica_groups=mesh['tx'=4,'ty'=8] {'tx'}, dimensions={1}, use_global_device_ids=true | all-gather | bytes 327680 | tf_op jit(solution)/shard_map/all_gather | solution.py:147
  74.1 35.2 %reduce-scatter.4.cloned.1.call-done = f32[128,320]{0,1:T(8,128)} async-done(((f32[128,2560]{0,1:T(8,128)}), f32[128,320]{0,1:T(8,128)}) %reduce-scatter.4.cloned.1.call-update) | async-done | bytes 163856 | tf_op jit(solution)/shard_map/reduce_scatter | solution.py:148
  115.8 7.7 %all-to-all-done = bf16[32,4,320]{2,1,0:T(4,128)(2,1)S(1)} async-done(((bf16[32,4,320]{2,1,0:T(4,128)(2,1)}), bf16[32,4,320]{2,1,0:T(4,128)(2,1)S(1)}, u32[]{:S(2)}, u32[]{:S(2)}) %all-to-all-start) | async-done | bytes 81952 | tf_op jit(solution)/shard_map/all_to_all | solution.py:157
  130.2 7.3 %all-to-all-done.1 = bf16[4,32,256]{2,0,1:T(4,128)(2,1)S(1)} async-done(((bf16[4,32,256]{2,0,1:T(4,128)(2,1)}), bf16[4,32,256]{2,0,1:T(4,128)(2,1)S(1)}, u32[]{:S(2)}, u32[]{:S(2)}) %all-to-all-start.1) | async-done | bytes 65568 | tf_op jit(solution)/shard_map/all_to_all | solution.py:170
  137.6 10.0 %all_gather.13 = bf16[128,2048]{1,0:T(8,128)(2,1)S(1)} all-gather(bf16[128,256]{1,0:T(8,128)(2,1)S(1)} %reshape.334), channel_id=1, replica_groups=mesh['tx'=4,'ty'=8] {'ty'}, dimensions={1}, use_global_device_ids=true | all-gather | bytes 589824 | tf_op jit(solution)/shard_map/all_gather | solution.py:177
  160.5 10.2 %reduce-scatter.6.cloned.1.call-done = f32[128,256]{1,0:T(8,128)} async-done(((f32[128,1024]{1,0:T(8,128)}), f32[128,256]{1,0:T(8,128)}) %reduce-scatter.6.cloned.1.call-update) | async-done | bytes 131088 | tf_op jit(solution)/shard_map/reduce_scatter | solution.py:178
  171.8 38.5 %psum.232 = f32[128]{0:T(128)S(1)} all-reduce(f32[128]{0:T(128)S(1)} %get-tuple-element.64), channel_id=1, replica_groups=mesh['tx'=4,'ty'=8] {'tx','ty'}, use_global_device_ids=true, to_apply=%region_10.11 | all-reduce | flops 128 | bytes 1024 | tf_op jit(solution)/shard_map/psum | solution.py:181
  210.4 14.4 %all_gather.14 = bf16[128,1024]{1,0:T(8,128)(2,1)S(1)} all-gather(bf16[128,256]{1,0:T(8,128)(2,1)S(1)} %fusion.54), channel_id=1, replica_groups=mesh['tx'=4,'ty'=8] {'tx'}, dimensions={1}, use_global_device_ids=true | all-gather | bytes 327680 | tf_op jit(solution)/shard_map/all_gather | solution.py:187
  225.8 33.3 %reduce-scatter.8.cloned.1.call-done = bf16[16,512]{1,0:T(8,128)(2,1)} async-done(((bf16[128,512]{1,0:T(8,128)(2,1)}), bf16[16,512]{1,0:T(8,128)(2,1)}) %reduce-scatter.8.cloned.1.call-update) | async-done | bytes 16400 | tf_op jit(solution)/shard_map/reduce_scatter | solution.py:188
  259.1 13.4 %all_gather.15 = bf16[16,2048]{1,0:T(8,128)(2,1)S(1)} all-gather(bf16[16,512]{1,0:T(8,128)(2,1)} %reduce-scatter.8.cloned.1.call-done), channel_id=1, replica_groups=mesh['tx'=4,'ty'=8] {'tx'}, dimensions={1}, use_global_device_ids=true | all-gather | bytes 81920 | tf_op jit(solution)/shard_map/all_gather | solution.py:191
  296.1 30.0 %all-reduce.32.cloned.1.call-done = (bf16[32,2048]{1,0:T(8,128)(2,1)}, bf16[32,2048]{1,0:T(8,128)(2,1)}) async-done(((bf16[32,2048]{1,0:T(8,128)(2,1)}, bf16[32,2048]{1,0:T(8,128)(2,1)}), (bf16[32,2048]{1,0:T(8,128)(2,1)}, bf16[32,2048]{1,0:T(8,128)(2,1)})) %all-reduce.32.cloned.1.call-update) | async-done | bytes 262160 | tf_op jit(solution)/shard_map/psum | solution.py:88
  330.4 5.8 convolution_convert_fusion.12
  338.1 33.6 %all-reduce.30.cloned.1.call-done = (bf16[32,2048]{1,0:T(8,128)(2,1)}, bf16[32,2048]{1,0:T(8,128)(2,1)}) async-done(((bf16[32,2048]{1,0:T(8,128)(2,1)}, bf16[32,2048]{1,0:T(8,128)(2,1)}), (bf16[32,2048]{1,0:T(8,128)(2,1)}, bf16[32,2048]{1,0:T(8,128)(2,1)})) %all-reduce.30.cloned.1.call-update) | async-done | bytes 262160 | tf_op jit(solution)/shard_map/psum | solution.py:88
  383.6 33.6 %all-reduce.28.cloned.1.call-done = (bf16[32,2048]{1,0:T(8,128)(2,1)}, bf16[32,2048]{1,0:T(8,128)(2,1)}) async-done(((bf16[32,2048]{1,0:T(8,128)(2,1)}, bf16[32,2048]{1,0:T(8,128)(2,1)}), (bf16[32,2048]{1,0:T(8,128)(2,1)}, bf16[32,2048]{1,0:T(8,128)(2,1)})) %all-reduce.28.cloned.1.call-update) | async-done | bytes 262160 | tf_op jit(solution)/shard_map/psum | solution.py:88
  421.4 5.8 convolution_convert_fusion.8
  429.0 33.6 %all-reduce.26.cloned.1.call-done = (bf16[32,2048]{1,0:T(8,128)(2,1)}, bf16[32,2048]{1,0:T(8,128)(2,1)}) async-done(((bf16[32,2048]{1,0:T(8,128)(2,1)}, bf16[32,2048]{1,0:T(8,128)(2,1)}), (bf16[32,2048]{1,0:T(8,128)(2,1)}, bf16[32,2048]{1,0:T(8,128)(2,1)})) %all-reduce.26.cloned.1.call-update) | async-done | bytes 262160 | tf_op jit(solution)/shard_map/psum | solution.py:88
  474.5 33.6 %all-reduce.24.cloned.1.call-done = (bf16[32,2048]{1,0:T(8,128)(2,1)}, bf16[32,2048]{1,0:T(8,128)(2,1)}) async-done(((bf16[32,2048]{1,0:T(8,128)(2,1)}, bf16[32,2048]{1,0:T(8,128)(2,1)}), (bf16[32,2048]{1,0:T(8,128)(2,1)}, bf16[32,2048]{1,0:T(8,128)(2,1)})) %all-reduce.24.cloned.1.call-update) | async-done | bytes 262160 | tf_op jit(solution)/shard_map/psum | solution.py:88
  520.2 33.4 %all-reduce.22.cloned.1.call-done = (bf16[32,2048]{1,0:T(8,128)(2,1)}, bf16[32,2048]{1,0:T(8,128)(2,1)}) async-done(((bf16[32,2048]{1,0:T(8,128)(2,1)}, bf16[32,2048]{1,0:T(8,128)(2,1)}), (bf16[32,2048]{1,0:T(8,128)(2,1)}, bf16[32,2048]{1,0:T(8,128)(2,1)})) %all-reduce.22.cloned.1.call-update) | async-done | bytes 262160 | tf_op jit(solution)/shard_map/psum | solution.py:88
  557.8 5.8 convolution_convert_fusion.2
  565.5 33.6 %all-reduce.20.cloned.1.call-done = (bf16[32,2048]{1,0:T(8,128)(2,1)}, bf16[32,2048]{1,0:T(8,128)(2,1)}) async-done(((bf16[32,2048]{1,0:T(8,128)(2,1)}, bf16[32,2048]{1,0:T(8,128)(2,1)}), (bf16[32,2048]{1,0:T(8,128)(2,1)}, bf16[32,2048]{1,0:T(8,128)(2,1)})) %all-reduce.20.cloned.1.call-update) | async-done | bytes 262160 | tf_op jit(solution)/shard_map/psum | solution.py:88
  611.0 10.7 %all-reduce.1 = (bf16[32]{0:T(256)(128)(2,1)S(1)}, bf16[32]{0:T(256)(128)(2,1)S(1)}, bf16[32]{0:T(256)(128)(2,1)S(1)}, bf16[32]{0:T(256)(128)(2,1)S(1)}, bf16[32...) all-reduce(bf16[32]{0:T(256)(128)(2,1)S(1)} %get-tuple-element.17, ...), channel_id=1, replica_groups=mesh['tx'=4,'ty'=8] {'tx'}, use_global_device_ids=true, to_apply=%region_18.19 | all-reduce | flops 448 | bytes 1792 | tf_op jit(solution)/shard_map/psum | solution.py:104
  621.8 23.6 %all-reduce.18.cloned.1.call-done = bf16[32,2048]{1,0:T(8,128)(2,1)} async-done(((bf16[32,2048]{1,0:T(8,128)(2,1)}), bf16[32,2048]{1,0:T(8,128)(2,1)}) %all-reduce.18.cloned.1.call-update) | async-done | bytes 131088 | tf_op jit(solution)/shard_map/psum | solution.py:88
  648.3 10.4 %all-reduce = (f32[32]{0:T(128)S(1)}, f32[32]{0:T(128)S(1)}) all-reduce(f32[32]{0:T(128)S(1)} %get-tuple-element.3, f32[32]{0:T(128)S(1)} %get-tuple-element.2), channel_id=1, replica_groups=mesh['tx'=4,'ty'=8] {'tx'}, use_global_device_ids=true, to_apply=%region_72.73 | all-reduce | flops 64 | bytes 512 | tf_op jit(solution)/shard_map/psum | solution.py:110
  (189 shorter events, 131.2 us)
Async XLA Ops:
  7.2 217.6 %copy-start = (bf16[1024,512]{1,0:T(8,128)(2,1)S(1)}, bf16[1024,512]{1,0:T(8,128)(2,1)}, u32[]{:S(2)}) copy-start(bf16[1024,512]{1,0:T(8,128)(2,1)} %param.27) | copy-start | bytes 3145732
  7.2 102.1 %reduce-scatter.4.cloned.1.call-start = ((), (), s32[]{:S(2)}) async-start(), calls=%async_computation.6 | async-start | bytes 1474560 | tf_op jit(solution)/shard_map/reduce_scatter | solution.py:148
  51.9 20.3 %copy-start.10 = (bf16[10240]{0:T(1024)(128)(2,1)S(1)}, bf16[10240]{0:T(1024)(128)(2,1)}, u32[]{:S(2)}) copy-start(bf16[10240]{0:T(1024)(128)(2,1)} %param.21) | copy-start | bytes 61444
  51.9 20.3 %copy-start.15 = (s32[4]{0:T(128)S(1)}, s32[4]{0:T(128)}, u32[]{:S(2)}) copy-start(s32[4]{0:T(128)} %param.24) | copy-start | bytes 52
  51.9 20.5 %copy-start.14 = (s32[128]{0:T(128)S(1)}, s32[128]{0:T(128)}, u32[]{:S(2)}) copy-start(s32[128]{0:T(128)} %param.28) | copy-start | bytes 1540
  72.2 52.2 %copy-start.1 = (bf16[4,128,1024]{2,1,0:T(8,128)(2,1)S(1)}, bf16[4,128,1024]{2,1,0:T(8,128)(2,1)}, u32[]{:S(2)}) copy-start(bf16[4,128,1024]{2,1,0:T(8,128)(2,1)} %param.22) | copy-start | bytes 3145732
  111.1 12.4 %all-to-all-start = ((bf16[32,4,320]{2,1,0:T(4,128)(2,1)}), bf16[32,4,320]{2,1,0:T(4,128)(2,1)S(1)}, u32[]{:S(2)}, u32[]{:S(2)}) async-start(bf16[32,4,320]{2,1,0:T(4,128)(2,1)} %copy.60), calls=%async_computation.1 | async-start | bytes 196608 | tf_op jit(solution)/shard_map/all_to_all | solution.py:157
  125.2 26.5 %copy-start.16 = (bf16[256]{0:T(256)(128)(2,1)S(1)}, bf16[256]{0:T(256)(128)(2,1)}, u32[]{:S(2)}) copy-start(bf16[256]{0:T(256)(128)(2,1)} %param.26) | copy-start | bytes 1540
  127.6 10.0 %all-to-all-start.1 = ((bf16[4,32,256]{2,0,1:T(4,128)(2,1)}), bf16[4,32,256]{2,0,1:T(4,128)(2,1)S(1)}, u32[]{:S(2)}, u32[]{:S(2)}) async-start(bf16[4,32,256]{2,0,1:T(4,128)(2,1)} %copy.64), calls=%async_computation.2 | async-start | bytes 131072 | tf_op jit(solution)/shard_map/all_to_all | solution.py:170
  130.1 40.6 %reduce-scatter.6.cloned.1.call-start = ((), (), s32[]{:S(2)}) async-start(), calls=%async_computation.7 | async-start | bytes 655360 | tf_op jit(solution)/shard_map/reduce_scatter | solution.py:178
  147.6 23.1 %copy-start.2 = (bf16[128,256]{1,0:T(8,128)(2,1)S(1)}, bf16[128,256]{1,0:T(8,128)(2,1)}, u32[]{:S(2)}) copy-start(bf16[128,256]{1,0:T(8,128)(2,1)} %param.18) | copy-start | bytes 196612
  151.4 107.7 %reduce-scatter.8.cloned.1.call-start = ((), (), s32[]{:S(2)}) async-start(), calls=%async_computation.8 | async-start | bytes 147456 | tf_op jit(solution)/shard_map/reduce_scatter | solution.py:188
  153.9 125.3 %copy-start.11 = (bf16[2048]{0:T(1024)(128)(2,1)S(1)}, bf16[2048]{0:T(1024)(128)(2,1)}, u32[]{:S(2)}) copy-start(bf16[2048]{0:T(1024)(128)(2,1)} %param.33) | copy-start | bytes 12292
  171.7 114.0 %copy-start.3 = (bf16[128,256]{1,0:T(8,128)(2,1)}, bf16[128,256]{1,0:T(8,128)(2,1)S(1)}, u32[]{:S(2)}) copy-start(bf16[128,256]{1,0:T(8,128)(2,1)S(1)} %get-tuple-element.65) | copy-start | bytes 196612
  273.5 8.8 %all-to-all-start.2 = ((bf16[8,4,2048]{2,1,0:T(4,128)(2,1)}), bf16[8,4,2048]{2,1,0:T(4,128)(2,1)S(1)}, u32[]{:S(2)}, u32[]{:S(2)}) async-start(bf16[8,4,2048]{2,1,0:T(4,128)(2,1)} %reshape.335), calls=%async_computation.5 | async-start | bytes 262144 | tf_op jit(solution)/shard_map/all_to_all | solution.py:206
  276.9 49.3 %all-reduce.32.cloned.1.call-start = ((), (), s32[]{:S(2)}) async-start(), calls=%async_computation.16 | async-start | bytes 524288 | tf_op jit(solution)/shard_map/psum | solution.py:88
  285.7 8.2 %copy-start.12 = (bf16[2048]{0:T(1024)(128)(2,1)S(1)}, bf16[2048]{0:T(1024)(128)(2,1)}, u32[]{:S(2)}) copy-start(bf16[2048]{0:T(1024)(128)(2,1)} %param.34) | copy-start | bytes 12292
  291.5 80.2 %all-reduce.30.cloned.1.call-start = ((), (), s32[]{:S(2)}) async-start(), calls=%async_computation.15 | async-start | bytes 524288 | tf_op jit(solution)/shard_map/psum | solution.py:88
  336.2 80.9 %all-reduce.28.cloned.1.call-start = ((), (), s32[]{:S(2)}) async-start(), calls=%async_computation.14 | async-start | bytes 524288 | tf_op jit(solution)/shard_map/psum | solution.py:88
  381.7 81.0 %all-reduce.26.cloned.1.call-start = ((), (), s32[]{:S(2)}) async-start(), calls=%async_computation.13 | async-start | bytes 524288 | tf_op jit(solution)/shard_map/psum | solution.py:88
  427.2 80.9 %all-reduce.24.cloned.1.call-start = ((), (), s32[]{:S(2)}) async-start(), calls=%async_computation.12 | async-start | bytes 524288 | tf_op jit(solution)/shard_map/psum | solution.py:88
  472.7 80.9 %all-reduce.22.cloned.1.call-start = ((), (), s32[]{:S(2)}) async-start(), calls=%async_computation.11 | async-start | bytes 524288 | tf_op jit(solution)/shard_map/psum | solution.py:88
  518.1 80.9 %all-reduce.20.cloned.1.call-start = ((), (), s32[]{:S(2)}) async-start(), calls=%async_computation.10 | async-start | bytes 524288 | tf_op jit(solution)/shard_map/psum | solution.py:88
  563.6 81.7 %all-reduce.18.cloned.1.call-start = ((), (), s32[]{:S(2)}) async-start(), calls=%async_computation.9 | async-start | bytes 262144 | tf_op jit(solution)/shard_map/psum | solution.py:88
  (7 other events, 42.9 us)
Sparse Core Ops, SparseCore 0:
  72.3 36.9 reduce-scatter.3
  151.6 19.1 reduce-scatter.5
  225.9 33.1 reduce-scatter.7
  291.6 34.5 all-reduce.31
  336.3 35.2 all-reduce.29
  381.8 35.2 all-reduce.27
  427.3 35.2 all-reduce.25
  472.8 35.2 all-reduce.23
  518.3 35.2 all-reduce.21
  563.8 35.2 all-reduce.19
  611.1 34.2 all-reduce.17
where the time goes:
time: 668 us; the launch traced here: 666 us
  waiting for transfers between devices  352 us (53%)
  blocking collectives  154 us (23%)
  matrix products  114 us (17%)
  other arithmetic  16.5 us (2%)
  between operations  14.5 us (2%)
  starting transfers between devices  11.4 us (2%)
    psum x8, waiting for transfers between devices, depth_rows(): lax.psum(down_part.astype(jnp.bfloat16), 'tx').astype(jnp.float32)  255 us
    dot_general x8, matrix products, depth_rows(): jnp.dot(activation, mlp_down, preferred_element_type=jnp.float32)  46.1 us
    psum x1, blocking collectives, body(): square_sum = lax.psum(jnp.sum(residual * residual, axis=1), ('tx', 'ty'))  42 us
    psum x1, blocking collectives, body(): final_sum = lax.psum(jnp.sum(leaving * leaving, axis=1), ('tx', 'ty'))  38.5 us
    reduce_scatter x1, waiting for transfers between devices, body(): lax.psum_scatter(partial_qkv, 'ty', scatter_dimension=1, tiled=True)  35.2 us
    reduce_scatter x1, waiting for transfers between devices, body(): lax.psum_scatter(partial_start.astype(jnp.bfloat16), 'ty', scatter_dimens...  33.3 us
    dot_general x8, matrix products, depth_rows(): jnp.dot(inner_rows, mlp_gate, preferred_element_type=jnp.float32)  24.5 us
    dot_general x7, matrix products, depth_rows(): jnp.dot(chosen.astype(jnp.bfloat16), table_rows, preferred_element_type=j...  15.4 us
  transfers between devices with their start and end apart: 14, of which 14 were waited for; matrix products, arithmetic and copies ran while one was open for 4% of the time, Pallas kernels for 0%

commit v1 on v0

v1 whole, which is shorter than its diff:
```python
import functools

import jax
import jax.numpy as jnp
from jax import lax
from jax.experimental import pallas as pl
from jax.experimental.pallas import tpu as pltpu
from jax.sharding import PartitionSpec as P

HEADS = 64
KV_HEADS = 8
HEAD_DIM = 128
STEPS = 8
LMAX = 128
LANES = 128
PAD = 16
VMEM_BYTES = 56 * 1024 * 1024
MESH = pl.DeviceIdType.MESH

epsilon = 1e-06
rope_base = 1000000.0
embed_gain = 16.0


def rotate(values, position):
    half_dim = values.shape[-1] // 2
    frequency = jnp.exp(
        -jnp.log(rope_base) * (2.0 * jnp.arange(half_dim, dtype=jnp.float32) / values.shape[-1])
    )
    phase_angle = position.astype(jnp.float32)[:, None, None] * frequency[None, None, :]
    cosine = jnp.cos(phase_angle)
    sine_part = jnp.sin(phase_angle)
    first_half = values[..., :half_dim]
    second_half = values[..., half_dim:]
    return jnp.concatenate(
        [
            first_half * cosine - second_half * sine_part,
            second_half * cosine + first_half * sine_part,
        ],
        axis=-1,
    )


def attend(query_heads, new_key, new_value, key_cache, value_cache, lengths):
    row_count = query_heads.shape[0]
    group_size = HEADS // KV_HEADS
    query_heads = query_heads.reshape(row_count, KV_HEADS, group_size, HEAD_DIM)
    keys_all = key_cache.reshape(row_count, LMAX, KV_HEADS, HEAD_DIM)
    values_all = value_cache.reshape(row_count, LMAX, KV_HEADS, HEAD_DIM)
    scores = jnp.einsum(
        "rgjd,rtgd->rgjt", query_heads, keys_all, preferred_element_type=jnp.float32
    )
    own_score = jnp.einsum(
        "rgjd,rgd->rgj", query_heads, new_key, preferred_element_type=jnp.float32
    )
    in_cache = jnp.arange(LMAX, dtype=jnp.int32)[None, :] < lengths[:, None]
    weights = jnp.where(in_cache[:, None, None, :], jnp.exp(scores), 0.0)
    own_weight = jnp.exp(own_score)
    denominator = jnp.sum(weights, axis=-1) + own_weight
    probability = (weights / denominator[..., None]).astype(jnp.bfloat16)
    own_prob = (own_weight / denominator).astype(jnp.bfloat16)
    blended = jnp.einsum(
        "rgjt,rtgd->rgjd", probability, values_all, preferred_element_type=jnp.float32
    )
    blended = (
        blended
        + own_prob.astype(jnp.float32)[..., None] * new_value.astype(jnp.float32)[:, :, None, :]
    )
    return blended.reshape(row_count, HEADS * HEAD_DIM).astype(jnp.bfloat16)


def split_square(total):
    total = jnp.broadcast_to(total, (total.shape[0], LANES))
    high = total.astype(jnp.bfloat16)
    low = (total - high.astype(jnp.float32)).astype(jnp.bfloat16)
    lane = lax.broadcasted_iota(jnp.int32, total.shape, 1)
    return jnp.where(lane < LANES // 2, high.astype(jnp.float32), low.astype(jnp.float32)).astype(
        jnp.bfloat16
    )


def join_square(block):
    block = block.astype(jnp.float32)
    return block[:, :1] + block[:, LANES // 2 : LANES // 2 + 1]


def push(source, target, send_sem, recv_sem, axis, peer):
    return pltpu.make_async_remote_copy(
        src_ref=source,
        dst_ref=target,
        send_sem=send_sem,
        recv_sem=recv_sem,
        device_id={axis: peer},
        device_id_type=MESH,
    )


def greet(axes):
    barrier = pltpu.get_barrier_semaphore()
    count = 0
    for axis in axes:
        me, size = lax.axis_index(axis), lax.axis_size(axis)
        for step in range(1, size):
            pl.semaphore_signal(
                barrier,
                inc=1,
                device_id={axis: lax.rem(me + step, size)},
                device_id_type=MESH,
            )
        count += size - 1
    pl.semaphore_wait(barrier, count)


def spread_own(buffer, send_sems, recv_sems, axis):
    me, size = lax.axis_index(axis), lax.axis_size(axis)
    for step in range(1, size):
        peer = lax.rem(me + step, size)
        push(
            buffer.at[me], buffer.at[me], send_sems.at[peer], recv_sems.at[me], axis, peer
        ).start()


def deal(source, buffer, send_sems, recv_sems, axis):
    me, size = lax.axis_index(axis), lax.axis_size(axis)
    for step in range(1, size):
        peer = lax.rem(me + step, size)
        push(
            source.at[peer], buffer.at[me], send_sems.at[peer], recv_sems.at[me], axis, peer
        ).start()


def take(buffer, send_sems, recv_sems, axis, step):
    me, size = lax.axis_index(axis), lax.axis_size(axis)
    peer = lax.rem(me + size - step, size)
    push(buffer.at[peer], buffer.at[peer], send_sems.at[peer], recv_sems.at[peer], axis, peer).wait_recv()
    return peer


def take_all(buffer, send_sems, recv_sems, axis):
    for step in range(1, lax.axis_size(axis)):
        take(buffer, send_sems, recv_sems, axis, step)


def settle(buffer, send_sems, recv_sems, axis):
    me, size = lax.axis_index(axis), lax.axis_size(axis)
    for step in range(1, size):
        peer = lax.rem(me + step, size)
        push(buffer.at[peer], buffer.at[peer], send_sems.at[peer], recv_sems.at[me], axis, peer).wait_send()


def gained_rows(blocks, rows, scaled_ref):
    square = jnp.zeros((rows, 1), jnp.float32)
    width = blocks.shape[2]
    for part in range(blocks.shape[0]):
        values = blocks[part, :rows, :].astype(jnp.float32)
        gain = blocks[part, rows : rows + PAD, :].astype(jnp.float32)[:1]
        square = square + jnp.sum(values * values, axis=1, keepdims=True)
        scaled_ref[:, part * width : (part + 1) * width] = (values * gain).astype(jnp.bfloat16)
    return square


def qkv_kernel(
    full_width, entry_ref, weight_hbm, out_ref, weight, gathered, scaled, sums_out, sums_in,
    rows_out, rows_in, weight_sem, g_send, g_recv, s_send, s_recv, r_send, r_recv,
):
    me_tx, me_ty = lax.axis_index("tx"), lax.axis_index("ty")
    count_tx, count_ty = lax.axis_size("tx"), lax.axis_size("ty")
    rows = scaled.shape[0]
    columns = weight.shape[1]
    fetch = pltpu.make_async_copy(weight_hbm, weight, weight_sem)
    fetch.start()
    gathered[me_tx] = entry_ref[...]
    greet(("tx", "ty"))
    spread_own(gathered, g_send, g_recv, "tx")
    take_all(gathered, g_send, g_recv, "tx")
    square = gained_rows(gathered, rows, scaled)
    fetch.wait()
    tile = 512
    block_rows = rows // count_ty
    for start in range(0, columns, tile):
        part = jnp.dot(
            scaled[...], weight[:, start : start + tile], preferred_element_type=jnp.float32
        )
        sums_out[:, :, start : start + tile] = part.astype(jnp.bfloat16).reshape(
            count_ty, block_rows, tile
        )
    sums_out[:, :, columns:] = split_square(square).reshape(count_ty, block_rows, LANES)
    deal(sums_out, sums_in, s_send, s_recv, "ty")
    sums_in[me_ty] = sums_out[me_ty]
    take_all(sums_in, s_send, s_recv, "ty")
    square = jnp.zeros((block_rows, 1), jnp.float32)
    for part in range(count_ty):
        square = square + join_square(sums_in[part, :, columns:])
    scale = lax.rsqrt(square / full_width + epsilon)
    own_rows = block_rows // count_tx
    piece = columns // count_tx
    raw = []
    for q in range(count_tx):
        total = jnp.zeros((block_rows, piece), jnp.float32)
        for part in range(count_ty):
            total = total + sums_in[part, :, q * piece : (q + 1) * piece].astype(jnp.float32)
        raw.append(total * scale)
    for d in range(count_tx):
        rows_out[d] = jnp.concatenate(
            [part[d * own_rows : (d + 1) * own_rows] for part in raw], axis=0
        ).astype(jnp.bfloat16)
    deal(rows_out, rows_in, r_send, r_recv, "tx")
    rows_in[me_tx] = rows_out[me_tx]
    take_all(rows_in, r_send, r_recv, "tx")
    out_ref[...] = rows_in[...]
    settle(gathered, g_send, g_recv, "tx")
    settle(sums_in, s_send, s_recv, "ty")
    settle(rows_in, r_send, r_recv, "tx")


def qkv_rows(entry, qkv_weight, rows, full_width, count_tx, count_ty):
    columns = qkv_weight.shape[1]
    block_rows = rows // count_ty
    piece = columns // count_tx
    dma = pltpu.SemaphoreType.DMA
    return pl.pallas_call(
        functools.partial(qkv_kernel, full_width),
        out_shape=jax.ShapeDtypeStruct((count_tx, block_rows, piece), jnp.bfloat16),
        in_specs=[
            pl.BlockSpec(memory_space=pltpu.VMEM),
            pl.BlockSpec(memory_space=pl.ANY),
        ],
        out_specs=pl.BlockSpec(memory_space=pltpu.VMEM),
        scratch_shapes=[
            pltpu.VMEM(qkv_weight.shape, jnp.bfloat16),
            pltpu.VMEM((count_tx,) + entry.shape, jnp.bfloat16),
            pltpu.VMEM((rows, count_tx * entry.shape[1]), jnp.bfloat16),
            pltpu.VMEM((count_ty, block_rows, columns + LANES), jnp.bfloat16),
            pltpu.VMEM((count_ty, block_rows, columns + LANES), jnp.bfloat16),
            pltpu.VMEM((count_tx, block_rows, piece), jnp.bfloat16),
            pltpu.VMEM((count_tx, block_rows, piece), jnp.bfloat16),
            dma,
            dma((count_tx,)), dma((count_tx,)),
            dma((count_ty,)), dma((count_ty,)),
            dma((count_tx,)), dma((count_tx,)),
        ],
        compiler_params=pltpu.CompilerParams(
            collective_id=1, has_side_effects=True, vmem_limit_bytes=VMEM_BYTES
        ),
    )(entry, qkv_weight)


def out_kernel(
    full_width, att_ref, out_hbm, resid_ref, gain_ref, in_hbm, select_ref, hidden_ref, state_ref,
    out_w, in_w, pieces, blocks, part_out, part_in, gathered, scaled, slots_out, slots_in,
    out_sem, in_sem, a_send, a_recv, b_send, b_recv, p_send, p_recv, g_send, g_recv, s_send, s_recv,
):
    me_tx, me_ty = lax.axis_index("tx"), lax.axis_index("ty")
    count_tx, count_ty = lax.axis_size("tx"), lax.axis_size("ty")
    rows, width = resid_ref.shape
    fetch_out = pltpu.make_async_copy(out_hbm, out_w, out_sem)
    fetch_out.start()
    fetch_in = pltpu.make_async_copy(in_hbm, in_w, in_sem)
    fetch_in.start()
    pieces[me_tx] = att_ref[me_tx]
    greet(("tx", "ty"))
    deal(att_ref, pieces, a_send, a_recv, "tx")
    take_all(pieces, a_send, a_recv, "tx")
    block_rows, piece = pieces.shape[1], pieces.shape[2]
    own_rows = block_rows // count_tx
    for q in range(count_tx):
        blocks[me_ty, :, q * piece : (q + 1) * piece] = jnp.concatenate(
            [
                pieces[src].astype(jnp.float32)[q * own_rows : (q + 1) * own_rows]
                for src in range(count_tx)
            ],
            axis=0,
        ).astype(jnp.bfloat16)
    spread_own(blocks, b_send, b_recv, "ty")
    take_all(blocks, b_send, b_recv, "ty")
    fetch_out.wait()
    attended = blocks[...].reshape(rows, blocks.shape[2])
    for d in range(count_tx):
        part_out[d] = jnp.dot(
            attended, out_w[:, d * width : (d + 1) * width], preferred_element_type=jnp.float32
        ).astype(jnp.bfloat16)
    deal(part_out, part_in, p_send, p_recv, "tx")
    part_in[me_tx] = part_out[me_tx]
    take_all(part_in, p_send, p_recv, "tx")
    total = resid_ref[...].astype(jnp.float32)
    for src in range(count_tx):
        total = total + part_in[src].astype(jnp.float32)
    hidden = total.astype(jnp.bfloat16)
    hidden_ref[...] = hidden
    gathered[me_tx, :rows, :] = hidden
    gathered[me_tx, rows:, :] = gain_ref[...]
    spread_own(gathered, g_send, g_recv, "tx")
    take_all(gathered, g_send, g_recv, "tx")
    square = gained_rows(gathered, rows, scaled)
    fetch_in.wait()
    start = jnp.dot(scaled[...], in_w[...], preferred_element_type=jnp.float32)
    message = jnp.concatenate([start.astype(jnp.bfloat16), split_square(square)], axis=1)
    slots = slots_out.shape[1]
    for owner in range(count_ty):
        slots_out[owner] = jnp.dot(
            select_ref[owner * slots : (owner + 1) * slots, :],
            message,
            preferred_element_type=jnp.float32,
        ).astype(jnp.bfloat16)
    deal(slots_out, slots_in, s_send, s_recv, "ty")
    slots_in[me_ty] = slots_out[me_ty]
    take_all(slots_in, s_send, s_recv, "ty")
    part_width = start.shape[1]
    total = jnp.zeros((slots, part_width), jnp.float32)
    square = jnp.zeros((slots, 1), jnp.float32)
    for src in range(count_ty):
        total = total + slots_in[src, :, :part_width].astype(jnp.float32)
        square = square + join_square(slots_in[src, :, part_width:])
    state_ref[...] = (
        (total * lax.rsqrt(square / full_width + epsilon)).astype(jnp.bfloat16).astype(jnp.float32)
    )
    settle(pieces, a_send, a_recv, "tx")
    settle(blocks, b_send, b_recv, "ty")
    settle(part_in, p_send, p_recv, "tx")
    settle(gathered, g_send, g_recv, "tx")
    settle(slots_in, s_send, s_recv, "ty")


def out_rows(
    attended, out_weight, residual, gain, in_weight, select, full_width, slots, count_tx, count_ty
):
    rows, width = residual.shape
    block_rows = attended.shape[1]
    columns = in_weight.shape[1]
    dma = pltpu.SemaphoreType.DMA
    inside = pl.BlockSpec(memory_space=pltpu.VMEM)
    outside = pl.BlockSpec(memory_space=pl.ANY)
    return pl.pallas_call(
        functools.partial(out_kernel, full_width),
        out_shape=(
            jax.ShapeDtypeStruct((rows, width), jnp.bfloat16),
            jax.ShapeDtypeStruct((slots, columns), jnp.float32),
        ),
        in_specs=[inside, outside, inside, inside, outside, inside],
        out_specs=(inside, inside),
        scratch_shapes=[
            pltpu.VMEM(out_weight.shape, jnp.bfloat16),
            pltpu.VMEM(in_weight.shape, jnp.bfloat16),
            pltpu.VMEM(attended.shape, jnp.bfloat16),
            pltpu.VMEM((count_ty, block_rows, out_weight.shape[0]), jnp.bfloat16),
            pltpu.VMEM((count_tx, rows, width), jnp.bfloat16),
            pltpu.VMEM((count_tx, rows, width), jnp.bfloat16),
            pltpu.VMEM((count_tx, rows + PAD, width), jnp.bfloat16),
            pltpu.VMEM((rows, count_tx * width), jnp.bfloat16),
            pltpu.VMEM((count_ty, slots, columns + LANES), jnp.bfloat16),
            pltpu.VMEM((count_ty, slots, columns + LANES), jnp.bfloat16),
            dma, dma,
            dma((count_tx,)), dma((count_tx,)),
            dma((count_ty,)), dma((count_ty,)),
            dma((count_tx,)), dma((count_tx,)),
            dma((count_tx,)), dma((count_tx,)),
            dma((count_ty,)), dma((count_ty,)),
        ],
        compiler_params=pltpu.CompilerParams(
            collective_id=2, has_side_effects=True, vmem_limit_bytes=VMEM_BYTES
        ),
    )(attended, out_weight, residual, gain, in_weight, select)


def depth_kernel(
    start_ref, codes_ref, pre_ref, head_ref, gate_hbm, up_hbm, down_hbm, table_hbm, out_ref,
    gate, up, down, table, state, gate_sum, up_sum, pre, out, sums_out, sums_in, words_out,
    words_in, ends, w_sem, pre_s, pre_r, out_s, out_r, sum_s, sum_r, word_s, word_r, end_s, end_r,
):
    me, count = lax.axis_index("tx"), lax.axis_size("tx")
    slots, width = start_ref.shape
    entries = table.shape[1]
    full = width * count
    fetches = [
        pltpu.make_async_copy(far, near, w_sem.at[i])
        for i, (far, near) in enumerate(
            ((gate_hbm, gate), (up_hbm, up), (down_hbm, down), (table_hbm, table))
        )
    ]
    for fetch in fetches:
        fetch.start()
    state[...] = start_ref[...]
    ends[me] = jnp.zeros(ends.shape[1:], jnp.float32)
    greet(("tx",))
    for fetch in fetches:
        fetch.wait()
    lane = lax.broadcasted_iota(jnp.int32, (slots, LANES), 1)
    entry = lax.broadcasted_iota(jnp.int32, (slots, entries), 1)

    def chosen(k):
        return codes_ref[k] - me * entries == entry

    def announce(buffer, k, gain_ref, send_sems, recv_sems):
        values = state[...]
        buffer[k, me, :, :width] = (values * gain_ref[...].astype(jnp.float32)).astype(jnp.bfloat16)
        buffer[k, me, :, width:] = split_square(jnp.sum(values * values, axis=1, keepdims=True))
        spread_own(buffer.at[k], send_sems.at[k], recv_sems.at[k], "tx")

    def score(k):
        logits = jnp.zeros((slots, entries), jnp.float32)
        square = jnp.zeros((slots, 1), jnp.float32)
        for step in range(count):
            if step:
                take(out.at[k], out_s.at[k], out_r.at[k], "tx", step)
            src = lax.rem(me + count - step, count)
            columns = pl.ds(pl.multiple_of(src * width, width), width)
            logits = logits + lax.dot_general(
                out[k, src, :, :width],
                table[k, :, columns],
                (((1,), (1,)), ((), ())),
                preferred_element_type=jnp.float32,
            )
            square = square + join_square(out[k, src, :, width:])
        logits = logits * lax.rsqrt(square / full + epsilon)
        total = jnp.sum(jnp.exp(logits), axis=1, keepdims=True)
        picked = jnp.sum(jnp.where(chosen(k), logits, 0.0), axis=1, keepdims=True)
        ends[me, 0] = jnp.where(lane == k, total, ends[me, 0])
        ends[me, 1] = jnp.where(lane == k, picked, ends[me, 1])

    def one_step(k, carry):
        announce(pre, k, pre_ref, pre_s, pre_r)

        @pl.when(k < STEPS - 1)
        def _():
            found = chosen(k).astype(jnp.float32).astype(jnp.bfloat16)
            for d in range(count):
                words_out[k, d] = jnp.dot(
                    found, table[k, :, d * width : (d + 1) * width],
                    preferred_element_type=jnp.float32,
                ).astype(jnp.bfloat16)
            deal(words_out.at[k], words_in.at[k], word_s.at[k], word_r.at[k], "tx")
            words_in[k, me] = words_out[k, me]

        square = jnp.zeros((slots, 1), jnp.float32)
        for step in range(count):
            if step:
                take(pre.at[k], pre_s.at[k], pre_r.at[k], "tx", step)
            src = lax.rem(me + count - step, count)
            depth = pl.ds(pl.multiple_of(src * width, width), width)
            block = pre[k, src, :, :width]
            gate_part = jnp.dot(block, gate[depth, :], preferred_element_type=jnp.float32)
            up_part = jnp.dot(block, up[depth, :], preferred_element_type=jnp.float32)
            if step:
                gate_part = gate_sum[...] + gate_part
                up_part = up_sum[...] + up_part
            gate_sum[...] = gate_part
            up_sum[...] = up_part
            square = square + join_square(pre[k, src, :, width:])
        scale = lax.rsqrt(square / full + epsilon)
        gate_part = gate_sum[...] * scale
        act = (gate_part / (1.0 + jnp.exp(-gate_part)) * (up_sum[...] * scale)).astype(jnp.bfloat16)
        for step in range(count - 1, -1, -1):
            peer = lax.rem(me + step, count)
            columns = pl.ds(pl.multiple_of(peer * width, width), width)
            part = jnp.dot(act, down[:, columns], preferred_element_type=jnp.float32)
            if step:
                sums_out[k, peer] = part.astype(jnp.bfloat16)
                push(
                    sums_out.at[k, peer], sums_in.at[k, me], sum_s.at[k, peer], sum_r.at[k, me],
                    "tx", peer,
                ).start()
            else:
                state[...] = state[...] + part

        @pl.when(k > 0)
        def _():
            score(k - 1)

        total = jnp.zeros((slots, width), jnp.float32)
        for step in range(1, count):
            src = take(sums_in.at[k], sum_s.at[k], sum_r.at[k], "tx", step)
            total = total + sums_in[k, src].astype(jnp.float32)
        state[...] = state[...] + total
        announce(out, k, head_ref, out_s, out_r)

        @pl.when(k < STEPS - 1)
        def _():
            word = words_in[k, me].astype(jnp.float32)
            for step in range(1, count):
                src = take(words_in.at[k], word_s.at[k], word_r.at[k], "tx", step)
                word = word + words_in[k, src].astype(jnp.float32)
            state[...] = state[...] + embed_gain * word

        return carry

    lax.fori_loop(0, STEPS, one_step, 0)
    score(STEPS - 1)
    spread_own(ends, end_s, end_r, "tx")
    take_all(ends, end_s, end_r, "tx")
    total = ends[0, 0]
    picked = ends[0, 1]
    for src in range(1, count):
        total = total + ends[src, 0]
        picked = picked + ends[src, 1]
    out_ref[...] = picked - jnp.log(jnp.where(lane < STEPS, total, 1.0))

    def close(k, carry):
        settle(pre.at[k], pre_s.at[k], pre_r.at[k], "tx")
        settle(out.at[k], out_s.at[k], out_r.at[k], "tx")
        settle(sums_in.at[k], sum_s.at[k], sum_r.at[k], "tx")

        @pl.when(k < STEPS - 1)
        def _():
            settle(words_in.at[k], word_s.at[k], word_r.at[k], "tx")

        return carry

    lax.fori_loop(0, STEPS, close, 0)
    settle(ends, end_s, end_r, "tx")


def depth_rows(start, codes, pre_gain, head_gain, mlp_gate, mlp_up, mlp_down, table, count_tx):
    slots, width = start.shape
    dma = pltpu.SemaphoreType.DMA
    inside = pl.BlockSpec(memory_space=pltpu.VMEM)
    outside = pl.BlockSpec(memory_space=pl.ANY)
    bf16, f32 = jnp.bfloat16, jnp.float32
    each = (STEPS, count_tx)
    return pl.pallas_call(
        depth_kernel,
        out_shape=jax.ShapeDtypeStruct((slots, LANES), f32),
        in_specs=[inside] * 4 + [outside] * 4,
        out_specs=inside,
        scratch_shapes=[
            pltpu.VMEM(mlp_gate.shape, bf16),
            pltpu.VMEM(mlp_up.shape, bf16),
            pltpu.VMEM(mlp_down.shape, bf16),
            pltpu.VMEM(table.shape, bf16),
            pltpu.VMEM((slots, width), f32),
            pltpu.VMEM((slots, mlp_gate.shape[1]), f32),
            pltpu.VMEM((slots, mlp_gate.shape[1]), f32),
            pltpu.VMEM(each + (slots, width + LANES), bf16),
            pltpu.VMEM(each + (slots, width + LANES), bf16),
            pltpu.VMEM(each + (slots, width), bf16),
            pltpu.VMEM(each + (slots, width), bf16),
            pltpu.VMEM(each + (slots, width), bf16),
            pltpu.VMEM(each + (slots, width), bf16),
            pltpu.VMEM((count_tx, 2, slots, LANES), f32),
            dma((4,)),
            dma(each), dma(each), dma(each), dma(each),
            dma(each), dma(each), dma(each), dma(each),
            dma((count_tx,)), dma((count_tx,)),
        ],
        compiler_params=pltpu.CompilerParams(
            collective_id=3, has_side_effects=True, vmem_limit_bytes=VMEM_BYTES
        ),
    )(start, codes, pre_gain, head_gain, mlp_gate, mlp_up, mlp_down, table)


def padded_gain(gain):
    return jnp.pad(gain[None, :], ((0, PAD - 1), (0, 0)))


def body(
    hidden_in,
    norm_gain,
    qkv_weight,
    qkv_bias,
    key_cache,
    value_cache,
    lengths,
    out_weight,
    final_gain,
    in_weight,
    owners,
    codebook_ids,
    mlp_gate,
    mlp_up,
    mlp_down,
    pre_gain,
    head_gain,
    codebook_table,
):
    count_tx = lax.axis_size("tx")
    count_ty = lax.axis_size("ty")
    batch_rows = hidden_in.shape[0]
    own_rows = key_cache.shape[0]
    block_rows = batch_rows // count_ty
    full_width = hidden_in.shape[1] * count_tx * count_ty
    entry = jnp.concatenate([hidden_in, padded_gain(norm_gain)], axis=0)
    raw = qkv_rows(entry, qkv_weight, batch_rows, full_width, count_tx, count_ty)
    qkv_raw = (
        raw.reshape(count_tx, count_tx, own_rows, raw.shape[2])
        .transpose(2, 0, 1, 3)
        .reshape(own_rows, count_tx * count_tx * raw.shape[2])
    )
    qkv = qkv_raw.astype(jnp.float32) + qkv_bias.astype(jnp.float32)
    query_width = HEADS * HEAD_DIM
    key_width = KV_HEADS * HEAD_DIM
    query_heads = rotate(qkv[:, :query_width].reshape(own_rows, HEADS, HEAD_DIM), lengths)
    query_heads = (query_heads * HEAD_DIM ** (-0.5)).astype(jnp.bfloat16)
    new_key = rotate(
        qkv[:, query_width : query_width + key_width].reshape(own_rows, KV_HEADS, HEAD_DIM), lengths
    ).astype(jnp.bfloat16)
    new_value = (
        qkv[:, query_width + key_width :].reshape(own_rows, KV_HEADS, HEAD_DIM).astype(jnp.bfloat16)
    )
    attended = attend(query_heads, new_key, new_value, key_cache, value_cache, lengths)
    attended = (
        attended.reshape(own_rows, count_tx, count_tx, -1)
        .transpose(1, 2, 0, 3)
        .reshape(count_tx, count_tx * own_rows, -1)
    )
    capacity = max(2, 2 * own_rows * count_tx // count_ty)
    slot_count = count_ty * capacity
    earlier = jnp.arange(block_rows)[:, None] > jnp.arange(block_rows)[None, :]
    same = owners.reshape(count_ty, block_rows, 1) == owners.reshape(count_ty, 1, block_rows)
    rank = jnp.sum((same & earlier[None]).astype(jnp.int32), axis=2)
    slot = (jnp.arange(count_ty, dtype=jnp.int32)[:, None] * capacity + rank).reshape(-1)
    place = owners * slot_count + slot
    select = (
        place[None, :] == jnp.arange(count_ty * slot_count, dtype=jnp.int32)[:, None]
    ).astype(jnp.bfloat16)
    hidden_out, start = out_rows(
        attended,
        out_weight,
        hidden_in,
        padded_gain(final_gain),
        in_weight,
        select,
        full_width,
        slot_count,
        count_tx,
        count_ty,
    )
    my_owner = lax.axis_index("ty")
    mine = place[None, :] == my_owner * slot_count + jnp.arange(slot_count, dtype=jnp.int32)[:, None]
    filled = jnp.any(mine, axis=1)
    codes = jnp.sum(jnp.where(mine[:, :, None], codebook_ids[None], 0), axis=1)
    codes = jnp.where(filled[:, None], codes, -1)
    width = start.shape[1]
    offset = lax.axis_index("tx") * width
    logprob = depth_rows(
        start,
        codes.T[:, :, None],
        lax.dynamic_slice_in_dim(pre_gain, offset, width)[None],
        lax.dynamic_slice_in_dim(head_gain, offset, width)[None],
        mlp_gate,
        mlp_up,
        mlp_down,
        codebook_table,
        count_tx,
    )
    logprob = jnp.where(filled[:, None], logprob[:, :STEPS], 0.0)
    return (hidden_out, logprob.T[None])


def solution(mesh):
    placed = (
        P(None, ("ty", "tx")),
        P(("ty", "tx")),
        P("ty", "tx"),
        P(),
        P(("ty", "tx"), None, None),
        P(("ty", "tx"), None, None),
        P(("ty", "tx")),
        P("tx", "ty"),
        P(("ty", "tx")),
        P("ty", "tx"),
        P(),
        P(),
        P(None, "tx"),
        P(None, "tx"),
        P("tx", None),
        P(),
        P(),
        P(None, "tx", None),
    )
    return jax.shard_map(
        body,
        mesh=mesh,
        in_specs=placed,
        out_specs=(P(None, ("ty", "tx")), P("ty", None, None)),
        check_vma=False,
    )
```

time: 668 us -> 215 us (0.32)
  waiting for transfers between devices: 352 us -> 0 us
  Pallas kernels: 0 us -> 199 us
  blocking collectives: 154 us -> 0 us
  matrix products: 114 us -> 1.31 us
  between operations: 14.5 us -> 0.88 us
  other arithmetic: 16.5 us -> 4.83 us
  starting transfers between devices: 11.4 us -> 0 us
    psum x8 -> x0, waiting for transfers between devices: 255 us -> none  [depth_rows(): lax.psum(down_part.astype(jnp.bfloat16), 'tx').astype(jnp.float32)]
    pallas_call x0 -> x3, Pallas kernels: none -> 199 us  [the longest x1 136 us: depth_rows(): pl.pallas_call(depth_kernel, out_shape=jax.ShapeDtypeStruct((slots, LANES...]
    dot_general x36 -> x0, matrix products: 111 us -> none  [the longest x8 46.1 us: depth_rows(): jnp.dot(activation, mlp_down, preferred_element_type=jnp.float32)]
    psum x4 -> x0, blocking collectives: 102 us -> none  [the longest x1 42 us: body(): square_sum = lax.psum(jnp.sum(residual * residual, axis=1), ('tx', 'ty'))]
    reduce_scatter x3 -> x0, waiting for transfers between devices: 78.7 us -> none  [the longest x1 35.2 us: body(): lax.psum_scatter(partial_qkv, 'ty', scatter_dimension=1, tiled=True)]
    all_gather x4 -> x0, blocking collectives: 52.4 us -> none  [the longest x1 14.5 us: body(): lax.all_gather(normed, 'tx', axis=1, tiled=True)]
    all_to_all x3 -> x0, waiting for transfers between devices: 18.3 us -> none  [the longest x1 7.74 us: body(): lax.all_to_all(ordered, ('tx', 'ty'), split_axis=0, concat_axis=1, tiled=...]
    reduce_sum x13 -> x2, other arithmetic: 11.5 us -> 0.9 us  [the longest x1 0.62 us: body(): codes = jnp.sum(jnp.where(mine[:, :, None], codebook_ids[None], 0), axis=1)]
  transfers between devices with their start and end apart: 14 -> 0, of which waited for: 14 -> 0; matrix products, arithmetic and copies ran while one was open for 4% -> 0% of each run, Pallas kernels for 0% -> 0%
where the time goes in v1:
time: 215 us; the launch traced here: 214 us
  Pallas kernels  199 us (93%)
  local copies, waits for them, and re-layouts  8.15 us (4%)
  other arithmetic  4.83 us (2%)
    pallas_call x1, Pallas kernels, depth_rows(): pl.pallas_call(depth_kernel, out_shape=jax.ShapeDtypeStruct((slots, LANES...  136 us
    pallas_call x1, Pallas kernels, out_rows(): pl.pallas_call(functools.partial(out_kernel, full_width), out_shape=(jax....  35.5 us
    pallas_call x1, Pallas kernels, qkv_rows(): pl.pallas_call(functools.partial(qkv_kernel, full_width), out_shape=jax.S...  27.3 us

profile of v1, /device:TPU:0, one launch (start us, length us, event | category | flops | bytes accessed | tf_op | source)
XLA Modules:
  0.0 214.3 jit_solution(10001824567936212422)
XLA Ops:
  0.7 0.7 broadcast_in_dim.96
  1.4 1.5 fusion.9.entry_ref
  2.9 27.3 %shard_map.185 = bf16[4,16,640]{2,1,0:T(8,128)(2,1)} custom-call(bf16[144,256]{1,0:T(8,128)(2,1)} %fusion.9.entry_ref, bf16[1024,2560]{1,0:T(8,128)(2,1)} %weight_hbm.1), custom_call_target="tpu_custom_call" | custom-call | tf_op jit(solution)/shard_map/pallas_call | solution.py:221
  30.2 0.9 reshape.185
  31.3 0.1 multiply_cosine_fusion
  31.9 0.2 fusion.11
  32.1 0.7 fusion.15
  32.9 0.4 fusion.1
  33.4 0.6 reshape.182.att_ref
  34.2 0.3 convert_reduce_fusion
  34.6 0.6 fusion.8.select_ref
  35.3 0.6 pad.8.gain_ref
  35.9 35.5 %shard_map.186 = (bf16[128,256]{1,0:T(8,128)(2,1)}, f32[32,512]{1,0:T(8,128)}) custom-call(bf16[4,16,512]{2,1,0:T(8,128)(2,1)} %reshape.182.att_ref, bf16[2048,1024]{1,0:T(8,128)(2,1)} %out_hbm.1, bf16[128,256]{1,0:T(8,128)(2,1)} %resid_ref.1, bf16[16,256]{1,0:T(8,128)(2,1)} %pad.8.gain_ref, bf16[1024,512]{1,0:T(8,128)(2,1)} %in_hbm.1, ...), custom_call_target="tpu_custom_call" | custom-call | tf_op jit(solution)/shard_map/pallas_call | solution.py:333
  71.4 0.8 dynamic_slice.6
  72.1 0.6 broadcast_in_dim.105.pre_ref
  72.7 0.8 dynamic_slice.7
  73.5 0.6 broadcast_in_dim.106.head_ref
  74.1 0.2 fusion.14
  74.2 0.6 select_reduce_fusion
  74.9 0.9 copy.36.codes_ref
  75.9 136.4 %shard_map.187 = f32[32,128]{1,0:T(8,128)} custom-call(f32[32,512]{1,0:T(8,128)} %get-tuple-element.5.start_ref, s32[8,32,1]{2,1,0:T(8,128)} %copy.36.codes_ref, bf16[1,512]{1,0:T(2,128)(2,1)} %broadcast_in_dim.105.pre_ref, bf16[1,512]{1,0:T(2,128)(2,1)} %broadcast_in_dim.106.head_ref, bf16[2048,1024]{1,0:T(8,128)(2,1)} %gate_hbm.1, ...), custom_call_target="tpu_custom_call" | custom-call | tf_op jit(solution)/shard_map/pallas_call | solution.py:519
  212.2 0.8 select_bitcast_fusion
  213.0 0.7 copy.37
  213.7 0.6 copy.68
  (43 shorter events, 1.1 us)
Async XLA Ops:
  0.6 31.4 %copy-start = (bf16[4,128,1024]{2,1,0:T(8,128)(2,1)S(1)}, bf16[4,128,1024]{2,1,0:T(8,128)(2,1)}, u32[]{:S(2)}) copy-start(bf16[4,128,1024]{2,1,0:T(8,128)(2,1)} %param.22) | copy-start | bytes 3145732
  0.6 30.5 %copy-start.2 = (bf16[10240]{0:T(1024)(128)(2,1)S(1)}, bf16[10240]{0:T(1024)(128)(2,1)}, u32[]{:S(2)}) copy-start(bf16[10240]{0:T(1024)(128)(2,1)} %param.21) | copy-start | bytes 61444
  0.7 30.6 %copy-start.6 = (s32[4]{0:T(128)S(1)}, s32[4]{0:T(128)}, u32[]{:S(2)}) copy-start(s32[4]{0:T(128)} %param.24) | copy-start | bytes 52
  2.9 30.0 %copy-start.5 = (bf16[4,128,1024]{2,1,0:T(8,128)(2,1)S(1)}, bf16[4,128,1024]{2,1,0:T(8,128)(2,1)}, u32[]{:S(2)}) copy-start(bf16[4,128,1024]{2,1,0:T(8,128)(2,1)} %param.23) | copy-start | bytes 3145732
  30.2 3.9 %copy-start.4 = (s32[128]{0:T(128)S(1)}, s32[128]{0:T(128)}, u32[]{:S(2)}) copy-start(s32[128]{0:T(128)} %param.28) | copy-start | bytes 1540
  30.2 5.1 %copy-start.7 = (bf16[256]{0:T(256)(128)(2,1)S(1)}, bf16[256]{0:T(256)(128)(2,1)}, u32[]{:S(2)}) copy-start(bf16[256]{0:T(256)(128)(2,1)} %param.26) | copy-start | bytes 1540
  32.8 41.4 %copy-start.3 = (s32[128,8]{0,1:T(8,128)S(1)}, s32[128,8]{0,1:T(8,128)}, u32[]{:S(2)}) copy-start(s32[128,8]{0,1:T(8,128)} %param.29) | copy-start | bytes 12292
  75.9 137.8 %copy-start.1 = (bf16[128,256]{1,0:T(8,128)(2,1)S(1)}, bf16[128,256]{1,0:T(8,128)(2,1)}, u32[]{:S(2)}) copy-start(bf16[128,256]{1,0:T(8,128)(2,1)} %get-tuple-element.24) | copy-start | bytes 196612

commit v2 on v1

--- a/solution.py
+++ b/solution.py
@@ -14,6 +14,7 @@
 LMAX = 128
 LANES = 128
 PAD = 16
+EARLY = 4
 VMEM_BYTES = 56 * 1024 * 1024
 MESH = pl.DeviceIdType.MESH
 
@@ -245,172 +246,141 @@
     )(entry, qkv_weight)
 
 
-def out_kernel(
-    full_width, att_ref, out_hbm, resid_ref, gain_ref, in_hbm, select_ref, hidden_ref, state_ref,
-    out_w, in_w, pieces, blocks, part_out, part_in, gathered, scaled, slots_out, slots_in,
-    out_sem, in_sem, a_send, a_recv, b_send, b_recv, p_send, p_recv, g_send, g_recv, s_send, s_recv,
+def tail_kernel(
+    full_width, att_ref, out_hbm, resid_ref, gain_ref, in_hbm, codes_ref, gains_ref, gate_hbm,
+    up_hbm, down_hbm, table_hbm, hidden_ref, out_ref,
+    out_w, in_w, gate, up, down, table, pieces, blocks, part_out, part_in, gathered, scaled,
+    starts_out, starts_in, state, gate_sum, up_sum, pre, out, sums_out, sums_in, words_out,
+    words_in, ends, finals,
+    w_sem, a_send, a_recv, b_send, b_recv, p_send, p_recv, g_send, g_recv, s_send, s_recv,
+    pre_s, pre_r, out_s, out_r, sum_s, sum_r, word_s, word_r, end_s, end_r, fin_s, fin_r,
 ):
-    me_tx, me_ty = lax.axis_index("tx"), lax.axis_index("ty")
-    count_tx, count_ty = lax.axis_size("tx"), lax.axis_size("ty")
-    rows, width = resid_ref.shape
-    fetch_out = pltpu.make_async_copy(out_hbm, out_w, out_sem)
-    fetch_out.start()
-    fetch_in = pltpu.make_async_copy(in_hbm, in_w, in_sem)
-    fetch_in.start()
-    pieces[me_tx] = att_ref[me_tx]
+    me, me_ty = lax.axis_index("tx"), lax.axis_index("ty")
+    count, count_ty = lax.axis_size("tx"), lax.axis_size("ty")
+    rows, feature_width = resid_ref.shape
+    block_rows, width = state.shape
+    entries = table.shape[1]
+    full = width * count
+    fetch_out, fetch_table, fetch_in, *fetch_rest = [
+        pltpu.make_async_copy(far, near, w_sem.at[i])
+        for i, (far, near) in enumerate(
+            (
+                (out_hbm, out_w),
+                (table_hbm, table),
+                (in_hbm, in_w),
+                (gate_hbm, gate),
+                (up_hbm, up),
+                (down_hbm, down),
+            )
+        )
+    ]
+    for fetch in [fetch_out, fetch_table, fetch_in] + fetch_rest:
+        fetch.start()
+    lane = lax.broadcasted_iota(jnp.int32, (block_rows, LANES), 1)
+    entry = lax.broadcasted_iota(jnp.int32, (block_rows, entries), 1)
+    codes = codes_ref[me_ty]
+    code_lane = lax.broadcasted_iota(jnp.int32, codes.shape, 1)
+
+    def chosen(k):
+        code = jnp.sum(jnp.where(code_lane == k, codes, 0), axis=1, keepdims=True)
+        return code - me * entries == entry
+
+    def send_words(k):
+        found = chosen(k).astype(jnp.float32).astype(jnp.bfloat16)
+        for d in range(count):
+            words_out[k, d] = jnp.dot(
+                found, table[k, :, d * width : (d + 1) * width], preferred_element_type=jnp.float32
+            ).astype(jnp.bfloat16)
+        deal(words_out.at[k], words_in.at[k], word_s.at[k], word_r.at[k], "tx")
+        words_in[k, me] = words_out[k, me]
+
+    pieces[me] = att_ref[me]
     greet(("tx", "ty"))
     deal(att_ref, pieces, a_send, a_recv, "tx")
     take_all(pieces, a_send, a_recv, "tx")
-    block_rows, piece = pieces.shape[1], pieces.shape[2]
-    own_rows = block_rows // count_tx
-    for q in range(count_tx):
+    piece = pieces.shape[2]
+    own_rows = block_rows // count
+    for q in range(count):
         blocks[me_ty, :, q * piece : (q + 1) * piece] = jnp.concatenate(
             [
                 pieces[src].astype(jnp.float32)[q * own_rows : (q + 1) * own_rows]
-                for src in range(count_tx)
+                for src in range(count)
             ],
             axis=0,
         ).astype(jnp.bfloat16)
     spread_own(blocks, b_send, b_recv, "ty")
+    fetch_table.wait()
+
+    def early_words(k, carry):
+        send_words(k)
+        return carry
+
+    lax.fori_loop(0, EARLY, early_words, 0)
     take_all(blocks, b_send, b_recv, "ty")
     fetch_out.wait()
     attended = blocks[...].reshape(rows, blocks.shape[2])
-    for d in range(count_tx):
+    for d in range(count):
         part_out[d] = jnp.dot(
-            attended, out_w[:, d * width : (d + 1) * width], preferred_element_type=jnp.float32
+            attended,
+            out_w[:, d * feature_width : (d + 1) * feature_width],
+            preferred_element_type=jnp.float32,
         ).astype(jnp.bfloat16)
     deal(part_out, part_in, p_send, p_recv, "tx")
-    part_in[me_tx] = part_out[me_tx]
+    part_in[me] = part_out[me]
     take_all(part_in, p_send, p_recv, "tx")
     total = resid_ref[...].astype(jnp.float32)
-    for src in range(count_tx):
+    for src in range(count):
         total = total + part_in[src].astype(jnp.float32)
     hidden = total.astype(jnp.bfloat16)
     hidden_ref[...] = hidden
-    gathered[me_tx, :rows, :] = hidden
-    gathered[me_tx, rows:, :] = gain_ref[...]
+    gathered[me, :rows, :] = hidden
+    gathered[me, rows:, :] = gain_ref[...]
     spread_own(gathered, g_send, g_recv, "tx")
     take_all(gathered, g_send, g_recv, "tx")
     square = gained_rows(gathered, rows, scaled)
     fetch_in.wait()
     start = jnp.dot(scaled[...], in_w[...], preferred_element_type=jnp.float32)
-    message = jnp.concatenate([start.astype(jnp.bfloat16), split_square(square)], axis=1)
-    slots = slots_out.shape[1]
-    for owner in range(count_ty):
-        slots_out[owner] = jnp.dot(
-            select_ref[owner * slots : (owner + 1) * slots, :],
-            message,
-            preferred_element_type=jnp.float32,
-        ).astype(jnp.bfloat16)
-    deal(slots_out, slots_in, s_send, s_recv, "ty")
-    slots_in[me_ty] = slots_out[me_ty]
-    take_all(slots_in, s_send, s_recv, "ty")
-    part_width = start.shape[1]
-    total = jnp.zeros((slots, part_width), jnp.float32)
-    square = jnp.zeros((slots, 1), jnp.float32)
+    starts_out[:, :, :width] = start.astype(jnp.bfloat16).reshape(count_ty, block_rows, width)
+    starts_out[:, :, width:] = split_square(square).reshape(count_ty, block_rows, LANES)
+    deal(starts_out, starts_in, s_send, s_recv, "ty")
+    starts_in[me_ty] = starts_out[me_ty]
+    ends[me] = jnp.zeros(ends.shape[1:], jnp.float32)
+    for fetch in fetch_rest:
+        fetch.wait()
+    take_all(starts_in, s_send, s_recv, "ty")
+    total = jnp.zeros((block_rows, width), jnp.float32)
+    square = jnp.zeros((block_rows, 1), jnp.float32)
     for src in range(count_ty):
-        total = total + slots_in[src, :, :part_width].astype(jnp.float32)
-        square = square + join_square(slots_in[src, :, part_width:])
-    state_ref[...] = (
-        (total * lax.rsqrt(square / full_width + epsilon)).astype(jnp.bfloat16).astype(jnp.float32)
-    )
-    settle(pieces, a_send, a_recv, "tx")
-    settle(blocks, b_send, b_recv, "ty")
-    settle(part_in, p_send, p_recv, "tx")
-    settle(gathered, g_send, g_recv, "tx")
-    settle(slots_in, s_send, s_recv, "ty")
-
-
-def out_rows(
-    attended, out_weight, residual, gain, in_weight, select, full_width, slots, count_tx, count_ty
-):
-    rows, width = residual.shape
-    block_rows = attended.shape[1]
-    columns = in_weight.shape[1]
-    dma = pltpu.SemaphoreType.DMA
-    inside = pl.BlockSpec(memory_space=pltpu.VMEM)
-    outside = pl.BlockSpec(memory_space=pl.ANY)
-    return pl.pallas_call(
-        functools.partial(out_kernel, full_width),
-        out_shape=(
-            jax.ShapeDtypeStruct((rows, width), jnp.bfloat16),
-            jax.ShapeDtypeStruct((slots, columns), jnp.float32),
-        ),
-        in_specs=[inside, outside, inside, inside, outside, inside],
-        out_specs=(inside, inside),
-        scratch_shapes=[
-            pltpu.VMEM(out_weight.shape, jnp.bfloat16),
-            pltpu.VMEM(in_weight.shape, jnp.bfloat16),
-            pltpu.VMEM(attended.shape, jnp.bfloat16),
-            pltpu.VMEM((count_ty, block_rows, out_weight.shape[0]), jnp.bfloat16),
-            pltpu.VMEM((count_tx, rows, width), jnp.bfloat16),
-            pltpu.VMEM((count_tx, rows, width), jnp.bfloat16),
-            pltpu.VMEM((count_tx, rows + PAD, width), jnp.bfloat16),
-            pltpu.VMEM((rows, count_tx * width), jnp.bfloat16),
-            pltpu.VMEM((count_ty, slots, columns + LANES), jnp.bfloat16),
-            pltpu.VMEM((count_ty, slots, columns + LANES), jnp.bfloat16),
-            dma, dma,
-            dma((count_tx,)), dma((count_tx,)),
-            dma((count_ty,)), dma((count_ty,)),
-            dma((count_tx,)), dma((count_tx,)),
-            dma((count_tx,)), dma((count_tx,)),
-            dma((count_ty,)), dma((count_ty,)),
-        ],
-        compiler_params=pltpu.CompilerParams(
-            collective_id=2, has_side_effects=True, vmem_limit_bytes=VMEM_BYTES
-        ),
-    )(attended, out_weight, residual, gain, in_weight, select)
-
-
-def depth_kernel(
-    start_ref, codes_ref, pre_ref, head_ref, gate_hbm, up_hbm, down_hbm, table_hbm, out_ref,
-    gate, up, down, table, state, gate_sum, up_sum, pre, out, sums_out, sums_in, words_out,
-    words_in, ends, w_sem, pre_s, pre_r, out_s, out_r, sum_s, sum_r, word_s, word_r, end_s, end_r,
-):
-    me, count = lax.axis_index("tx"), lax.axis_size("tx")
-    slots, width = start_ref.shape
-    entries = table.shape[1]
-    full = width * count
-    fetches = [
-        pltpu.make_async_copy(far, near, w_sem.at[i])
-        for i, (far, near) in enumerate(
-            ((gate_hbm, gate), (up_hbm, up), (down_hbm, down), (table_hbm, table))
-        )
-    ]
-    for fetch in fetches:
-        fetch.start()
-    state[...] = start_ref[...]
-    ends[me] = jnp.zeros(ends.shape[1:], jnp.float32)
-    greet(("tx",))
-    for fetch in fetches:
-        fetch.wait()
-    lane = lax.broadcasted_iota(jnp.int32, (slots, LANES), 1)
-    entry = lax.broadcasted_iota(jnp.int32, (slots, entries), 1)
-
-    def chosen(k):
-        return codes_ref[k] - me * entries == entry
-
-    def announce(buffer, k, gain_ref, send_sems, recv_sems):
-        values = state[...]
-        buffer[k, me, :, :width] = (values * gain_ref[...].astype(jnp.float32)).astype(jnp.bfloat16)
-        buffer[k, me, :, width:] = split_square(jnp.sum(values * values, axis=1, keepdims=True))
+        total = total + starts_in[src, :, :width].astype(jnp.float32)
+        square = square + join_square(starts_in[src, :, width:])
+    scale = lax.rsqrt(square / full_width + epsilon)
+    state[...] = (total * scale).astype(jnp.bfloat16).astype(jnp.float32)
+
+    def announce(buffer, k, values, send_sems, recv_sems):
+        buffer[k, me] = values.astype(jnp.bfloat16)
         spread_own(buffer.at[k], send_sems.at[k], recv_sems.at[k], "tx")
 
+    def gained(buffer, k, src, which):
+        values = buffer[k, src].astype(jnp.float32)
+        square = jnp.sum(values * values, axis=1, keepdims=True)
+        return (values * gains_ref[which, src]).astype(jnp.bfloat16), square
+
     def score(k):
-        logits = jnp.zeros((slots, entries), jnp.float32)
-        square = jnp.zeros((slots, 1), jnp.float32)
+        logits = jnp.zeros((block_rows, entries), jnp.float32)
+        square = jnp.zeros((block_rows, 1), jnp.float32)
         for step in range(count):
             if step:
                 take(out.at[k], out_s.at[k], out_r.at[k], "tx", step)
             src = lax.rem(me + count - step, count)
             columns = pl.ds(pl.multiple_of(src * width, width), width)
+            block, term = gained(out, k, src, 1)
             logits = logits + lax.dot_general(
-                out[k, src, :, :width],
+                block,
                 table[k, :, columns],
                 (((1,), (1,)), ((), ())),
                 preferred_element_type=jnp.float32,
             )
-            square = square + join_square(out[k, src, :, width:])
+            square = square + term
         logits = logits * lax.rsqrt(square / full + epsilon)
         total = jnp.sum(jnp.exp(logits), axis=1, keepdims=True)
         picked = jnp.sum(jnp.where(chosen(k), logits, 0.0), axis=1, keepdims=True)
@@ -418,26 +388,17 @@
         ends[me, 1] = jnp.where(lane == k, picked, ends[me, 1])
 
     def one_step(k, carry):
-        announce(pre, k, pre_ref, pre_s, pre_r)
-
-        @pl.when(k < STEPS - 1)
+        @pl.when(k < STEPS - 1 - EARLY)
         def _():
-            found = chosen(k).astype(jnp.float32).astype(jnp.bfloat16)
-            for d in range(count):
-                words_out[k, d] = jnp.dot(
-                    found, table[k, :, d * width : (d + 1) * width],
-                    preferred_element_type=jnp.float32,
-                ).astype(jnp.bfloat16)
-            deal(words_out.at[k], words_in.at[k], word_s.at[k], word_r.at[k], "tx")
-            words_in[k, me] = words_out[k, me]
-
-        square = jnp.zeros((slots, 1), jnp.float32)
+            send_words(k + EARLY)
+
+        square = jnp.zeros((block_rows, 1), jnp.float32)
         for step in range(count):
             if step:
                 take(pre.at[k], pre_s.at[k], pre_r.at[k], "tx", step)
             src = lax.rem(me + count - step, count)
             depth = pl.ds(pl.multiple_of(src * width, width), width)
-            block = pre[k, src, :, :width]
+            block, term = gained(pre, k, src, 0)
             gate_part = jnp.dot(block, gate[depth, :], preferred_element_type=jnp.float32)
             up_part = jnp.dot(block, up[depth, :], preferred_element_type=jnp.float32)
             if step:
@@ -445,7 +406,7 @@
                 up_part = up_sum[...] + up_part
             gate_sum[...] = gate_part
             up_sum[...] = up_part
-            square = square + join_square(pre[k, src, :, width:])
+            square = square + term
         scale = lax.rsqrt(square / full + epsilon)
         gate_part = gate_sum[...] * scale
         act = (gate_part / (1.0 + jnp.exp(-gate_part)) * (up_sum[...] * scale)).astype(jnp.bfloat16)
@@ -466,12 +427,11 @@
         def _():
             score(k - 1)
 
-        total = jnp.zeros((slots, width), jnp.float32)
+        total = jnp.zeros((block_rows, width), jnp.float32)
         for step in range(1, count):
             src = take(sums_in.at[k], sum_s.at[k], sum_r.at[k], "tx", step)
             total = total + sums_in[k, src].astype(jnp.float32)
-        state[...] = state[...] + total
-        announce(out, k, head_ref, out_s, out_r)
+        settled = state[...] + total
 
         @pl.when(k < STEPS - 1)
         def _():
@@ -479,10 +439,14 @@
             for step in range(1, count):
                 src = take(words_in.at[k], word_s.at[k], word_r.at[k], "tx", step)
                 word = word + words_in[k, src].astype(jnp.float32)
-            state[...] = state[...] + embed_gain * word
-
+            entering = settled + embed_gain * word
+            state[...] = entering
+            announce(pre, k + 1, entering, pre_s, pre_r)
+
+        announce(out, k, settled, out_s, out_r)
         return carry
 
+    announce(pre, 0, state[...], pre_s, pre_r)
     lax.fori_loop(0, STEPS, one_step, 0)
     score(STEPS - 1)
     spread_own(ends, end_s, end_r, "tx")
@@ -492,7 +456,15 @@
     for src in range(1, count):
         total = total + ends[src, 0]
         picked = picked + ends[src, 1]
-    out_ref[...] = picked - jnp.log(jnp.where(lane < STEPS, total, 1.0))
+    finals[me_ty] = picked - jnp.log(jnp.where(lane < STEPS, total, 1.0))
+    spread_own(finals, fin_s, fin_r, "ty")
+    take_all(finals, fin_s, fin_r, "ty")
+    out_ref[...] = finals[...]
+    settle(pieces, a_send, a_recv, "tx")
+    settle(blocks, b_send, b_recv, "ty")
+    settle(part_in, p_send, p_recv, "tx")
+    settle(gathered, g_send, g_recv, "tx")
+    settle(starts_in, s_send, s_recv, "ty")
 
     def close(k, carry):
         settle(pre.at[k], pre_s.at[k], pre_r.at[k], "tx")
@@ -507,44 +479,66 @@
 
     lax.fori_loop(0, STEPS, close, 0)
     settle(ends, end_s, end_r, "tx")
-
-
-def depth_rows(start, codes, pre_gain, head_gain, mlp_gate, mlp_up, mlp_down, table, count_tx):
-    slots, width = start.shape
+    settle(finals, fin_s, fin_r, "ty")
+
+
+def tail_rows(
+    attended, out_weight, residual, gain, in_weight, codes, gains, mlp_gate, mlp_up, mlp_down,
+    table, full_width, count_tx, count_ty,
+):
+    rows, width = residual.shape
+    block_rows = attended.shape[1]
+    columns = in_weight.shape[1]
+    hidden_units = mlp_gate.shape[1]
     dma = pltpu.SemaphoreType.DMA
     inside = pl.BlockSpec(memory_space=pltpu.VMEM)
     outside = pl.BlockSpec(memory_space=pl.ANY)
     bf16, f32 = jnp.bfloat16, jnp.float32
     each = (STEPS, count_tx)
+    by_tx, by_ty = dma((count_tx,)), dma((count_ty,))
     return pl.pallas_call(
-        depth_kernel,
-        out_shape=jax.ShapeDtypeStruct((slots, LANES), f32),
-        in_specs=[inside] * 4 + [outside] * 4,
-        out_specs=inside,
+        functools.partial(tail_kernel, full_width),
+        out_shape=(
+            jax.ShapeDtypeStruct((rows, width), bf16),
+            jax.ShapeDtypeStruct((count_ty, block_rows, LANES), f32),
+        ),
+        in_specs=[inside, outside, inside, inside, outside, inside, inside] + [outside] * 4,
+        out_specs=(inside, inside),
         scratch_shapes=[
+            pltpu.VMEM(out_weight.shape, bf16),
+            pltpu.VMEM(in_weight.shape, bf16),
             pltpu.VMEM(mlp_gate.shape, bf16),
             pltpu.VMEM(mlp_up.shape, bf16),
             pltpu.VMEM(mlp_down.shape, bf16),
             pltpu.VMEM(table.shape, bf16),
-            pltpu.VMEM((slots, width), f32),
-            pltpu.VMEM((slots, mlp_gate.shape[1]), f32),
-            pltpu.VMEM((slots, mlp_gate.shape[1]), f32),
-            pltpu.VMEM(each + (slots, width + LANES), bf16),
-            pltpu.VMEM(each + (slots, width + LANES), bf16),
-            pltpu.VMEM(each + (slots, width), bf16),
-            pltpu.VMEM(each + (slots, width), bf16),
-            pltpu.VMEM(each + (slots, width), bf16),
-            pltpu.VMEM(each + (slots, width), bf16),
-            pltpu.VMEM((count_tx, 2, slots, LANES), f32),
-            dma((4,)),
-            dma(each), dma(each), dma(each), dma(each),
-            dma(each), dma(each), dma(each), dma(each),
-            dma((count_tx,)), dma((count_tx,)),
-        ],
+            pltpu.VMEM(attended.shape, bf16),
+            pltpu.VMEM((count_ty, block_rows, out_weight.shape[0]), bf16),
+            pltpu.VMEM((count_tx, rows, width), bf16),
+            pltpu.VMEM((count_tx, rows, width), bf16),
+            pltpu.VMEM((count_tx, rows + PAD, width), bf16),
+            pltpu.VMEM((rows, count_tx * width), bf16),
+            pltpu.VMEM((count_ty, block_rows, columns + LANES), bf16),
+            pltpu.VMEM((count_ty, block_rows, columns + LANES), bf16),
+            pltpu.VMEM((block_rows, columns), f32),
+            pltpu.VMEM((block_rows, hidden_units), f32),
+            pltpu.VMEM((block_rows, hidden_units), f32),
+        ]
+        + [pltpu.VMEM(each + (block_rows, columns), bf16)] * 6
+        + [
+            pltpu.VMEM((count_tx, 2, block_rows, LANES), f32),
+            pltpu.VMEM((count_ty, block_rows, LANES), f32),
+            dma((6,)),
+            by_tx, by_tx, by_ty, by_ty, by_tx, by_tx, by_tx, by_tx, by_ty, by_ty,
+        ]
+        + [dma(each)] * 8
+        + [by_tx, by_tx, by_ty, by_ty],
         compiler_params=pltpu.CompilerParams(
-            collective_id=3, has_side_effects=True, vmem_limit_bytes=VMEM_BYTES
+            collective_id=2, has_side_effects=True, vmem_limit_bytes=VMEM_BYTES
         ),
-    )(start, codes, pre_gain, head_gain, mlp_gate, mlp_up, mlp_down, table)
+    )(
+        attended, out_weight, residual, gain, in_weight, codes, gains, mlp_gate, mlp_up, mlp_down,
+        table,
+    )
 
 
 def padded_gain(gain):
@@ -601,48 +595,35 @@
         .transpose(1, 2, 0, 3)
         .reshape(count_tx, count_tx * own_rows, -1)
     )
+    width = in_weight.shape[1]
+    gains = jnp.stack([pre_gain, head_gain]).astype(jnp.float32)
+    hidden_out, logprob = tail_rows(
+        attended,
+        out_weight,
+        hidden_in,
+        padded_gain(final_gain),
+        in_weight,
+        codebook_ids.reshape(count_ty, block_rows, STEPS),
+        gains.reshape(2, count_tx, 1, width),
+        mlp_gate,
+        mlp_up,
+        mlp_down,
+        codebook_table,
+        full_width,
+        count_tx,
+        count_ty,
+    )
     capacity = max(2, 2 * own_rows * count_tx // count_ty)
     slot_count = count_ty * capacity
     earlier = jnp.arange(block_rows)[:, None] > jnp.arange(block_rows)[None, :]
     same = owners.reshape(count_ty, block_rows, 1) == owners.reshape(count_ty, 1, block_rows)
     rank = jnp.sum((same & earlier[None]).astype(jnp.int32), axis=2)
     slot = (jnp.arange(count_ty, dtype=jnp.int32)[:, None] * capacity + rank).reshape(-1)
-    place = owners * slot_count + slot
-    select = (
-        place[None, :] == jnp.arange(count_ty * slot_count, dtype=jnp.int32)[:, None]
-    ).astype(jnp.bfloat16)
-    hidden_out, start = out_rows(
-        attended,
-        out_weight,
-        hidden_in,
-        padded_gain(final_gain),
-        in_weight,
-        select,
-        full_width,
-        slot_count,
-        count_tx,
-        count_ty,
-    )
-    my_owner = lax.axis_index("ty")
-    mine = place[None, :] == my_owner * slot_count + jnp.arange(slot_count, dtype=jnp.int32)[:, None]
-    filled = jnp.any(mine, axis=1)
-    codes = jnp.sum(jnp.where(mine[:, :, None], codebook_ids[None], 0), axis=1)
-    codes = jnp.where(filled[:, None], codes, -1)
-    width = start.shape[1]
-    offset = lax.axis_index("tx") * width
-    logprob = depth_rows(
-        start,
-        codes.T[:, :, None],
-        lax.dynamic_slice_in_dim(pre_gain, offset, width)[None],
-        lax.dynamic_slice_in_dim(head_gain, offset, width)[None],
-        mlp_gate,
-        mlp_up,
-        mlp_down,
-        codebook_table,
-        count_tx,
-    )
-    logprob = jnp.where(filled[:, None], logprob[:, :STEPS], 0.0)
-    return (hidden_out, logprob.T[None])
+    place = jnp.where(owners == lax.axis_index("ty"), slot, -1)
+    mine = place[None, :] == jnp.arange(slot_count, dtype=jnp.int32)[:, None]
+    logprob = logprob.reshape(batch_rows, LANES)[:, :STEPS].T
+    placed_rows = jnp.sum(jnp.where(mine[None], logprob[:, None, :], 0.0), axis=2)
+    return (hidden_out, placed_rows[None])
 
 
 def solution(mesh):

time: 215 us -> 168 us (0.78)
  Pallas kernels: 199 us -> 149 us
    pallas_call x2 -> x1, Pallas kernels: 172 us -> 122 us  [tail_rows(): pl.pallas_call(functools.partial(tail_kernel, full_width), out_shape=(jax...]
where the time goes in v2:
time: 168 us; the launch traced here: 167 us
  Pallas kernels  149 us (89%)
  local copies, waits for them, and re-layouts  9.61 us (6%)
  other arithmetic  6.65 us (4%)
    pallas_call x1, Pallas kernels, tail_rows(): pl.pallas_call(functools.partial(tail_kernel, full_width), out_shape=(jax...  122 us
    pallas_call x1, Pallas kernels, qkv_rows(): pl.pallas_call(functools.partial(qkv_kernel, full_width), out_shape=jax.S...  27.3 us

profile of v2, /device:TPU:0, one launch (start us, length us, event | category | flops | bytes accessed | tf_op | source)
XLA Modules:
  0.0 167.4 jit_solution(10561455031660539480)
XLA Ops:
  0.6 0.7 convert_element_type.77
  1.4 0.7 iota_compare_fusion.3
  2.1 0.7 broadcast_in_dim.36
  2.8 0.7 broadcast_in_dim.45
  3.6 0.7 eq.40
  4.3 0.3 convert_reduce_fusion
  4.8 0.7 compare_select_fusion
  5.4 0.6 pad.8.gain_ref
  6.0 0.7 stack.12
  6.7 0.7 stack.13
  7.4 0.6 maximum_convert_fusion.gains_ref
  8.1 0.7 convert_element_type.76
  8.8 1.4 copy.35
  10.2 1.5 fusion.8.entry_ref
  11.7 27.3 %shard_map.185 = bf16[4,16,640]{2,1,0:T(8,128)(2,1)} custom-call(bf16[144,256]{1,0:T(8,128)(2,1)} %fusion.8.entry_ref, bf16[1024,2560]{1,0:T(8,128)(2,1)} %weight_hbm.1), custom_call_target="tpu_custom_call" | custom-call | tf_op jit(solution)/shard_map/pallas_call | solution.py:222
  39.0 0.9 reshape.215
  40.4 0.1 fusion.10
  40.6 0.7 fusion.13
  41.4 0.4 fusion.1
  41.9 0.6 reshape.210.att_ref
  42.6 121.8 %shard_map.186 = (bf16[128,256]{1,0:T(8,128)(2,1)}, f32[8,16,128]{2,1,0:T(8,128)}) custom-call(bf16[4,16,512]{2,1,0:T(8,128)(2,1)} %reshape.210.att_ref, bf16[2048,1024]{1,0:T(8,128)(2,1)} %out_hbm.1, bf16[128,256]{1,0:T(8,128)(2,1)} %resid_ref.1, bf16[16,256]{1,0:T(8,128)(2,1)} %pad.8.gain_ref, bf16[1024,512]{1,0:T(8,128)(2,1)} %in_hbm.1, ...), custom_call_target="tpu_custom_call" | custom-call | tf_op jit(solution)/shard_map/pallas_call | solution.py:499
  164.3 0.8 slice_bitcast_fusion.1
  165.2 0.7 select_reduce_fusion
  166.0 1.5 copy.67
  (26 shorter events, 0.9 us)
Async XLA Ops:
  0.6 40.0 %copy-start = (bf16[4,128,1024]{2,1,0:T(8,128)(2,1)S(1)}, bf16[4,128,1024]{2,1,0:T(8,128)(2,1)}, u32[]{:S(2)}) copy-start(bf16[4,128,1024]{2,1,0:T(8,128)(2,1)} %param.22) | copy-start | bytes 3145732
  11.7 29.7 %copy-start.1 = (bf16[4,128,1024]{2,1,0:T(8,128)(2,1)S(1)}, bf16[4,128,1024]{2,1,0:T(8,128)(2,1)}, u32[]{:S(2)}) copy-start(bf16[4,128,1024]{2,1,0:T(8,128)(2,1)} %param.23) | copy-start | bytes 3145732

commit v3 on v2

--- a/solution.py
+++ b/solution.py
@@ -14,7 +14,6 @@
 LMAX = 128
 LANES = 128
 PAD = 16
-EARLY = 4
 VMEM_BYTES = 56 * 1024 * 1024
 MESH = pl.DeviceIdType.MESH
 
@@ -96,44 +95,51 @@
     )
 
 
+def partner(axis, step):
+    me, size = lax.axis_index(axis), lax.axis_size(axis)
+    other, bit = me, 1
+    while bit < size:
+        if (step // bit) % 2:
+            other = other + bit - 2 * bit * lax.rem(me // bit, 2)
+        bit *= 2
+    return other
+
+
 def greet(axes):
     barrier = pltpu.get_barrier_semaphore()
     count = 0
     for axis in axes:
-        me, size = lax.axis_index(axis), lax.axis_size(axis)
-        for step in range(1, size):
+        for step in range(1, lax.axis_size(axis)):
             pl.semaphore_signal(
-                barrier,
-                inc=1,
-                device_id={axis: lax.rem(me + step, size)},
-                device_id_type=MESH,
+                barrier, inc=1, device_id={axis: partner(axis, step)}, device_id_type=MESH
             )
-        count += size - 1
+        count += lax.axis_size(axis) - 1
     pl.semaphore_wait(barrier, count)
 
 
 def spread_own(buffer, send_sems, recv_sems, axis):
-    me, size = lax.axis_index(axis), lax.axis_size(axis)
-    for step in range(1, size):
-        peer = lax.rem(me + step, size)
+    me = lax.axis_index(axis)
+    for step in range(lax.axis_size(axis) - 1, 0, -1):
+        peer = partner(axis, step)
         push(
             buffer.at[me], buffer.at[me], send_sems.at[peer], recv_sems.at[me], axis, peer
         ).start()
 
 
 def deal(source, buffer, send_sems, recv_sems, axis):
-    me, size = lax.axis_index(axis), lax.axis_size(axis)
-    for step in range(1, size):
-        peer = lax.rem(me + step, size)
+    me = lax.axis_index(axis)
+    for step in range(lax.axis_size(axis) - 1, 0, -1):
+        peer = partner(axis, step)
         push(
             source.at[peer], buffer.at[me], send_sems.at[peer], recv_sems.at[me], axis, peer
         ).start()
 
 
 def take(buffer, send_sems, recv_sems, axis, step):
-    me, size = lax.axis_index(axis), lax.axis_size(axis)
-    peer = lax.rem(me + size - step, size)
-    push(buffer.at[peer], buffer.at[peer], send_sems.at[peer], recv_sems.at[peer], axis, peer).wait_recv()
+    peer = partner(axis, step)
+    push(
+        buffer.at[peer], buffer.at[peer], send_sems.at[peer], recv_sems.at[peer], axis, peer
+    ).wait_recv()
     return peer
 
 
@@ -143,10 +149,22 @@
 
 
 def settle(buffer, send_sems, recv_sems, axis):
-    me, size = lax.axis_index(axis), lax.axis_size(axis)
-    for step in range(1, size):
-        peer = lax.rem(me + step, size)
-        push(buffer.at[peer], buffer.at[peer], send_sems.at[peer], recv_sems.at[me], axis, peer).wait_send()
+    me = lax.axis_index(axis)
+    for step in range(1, lax.axis_size(axis)):
+        peer = partner(axis, step)
+        push(
+            buffer.at[peer], buffer.at[peer], send_sems.at[peer], recv_sems.at[me], axis, peer
+        ).wait_send()
+
+
+def spread_gain(gain_ref):
+    return jnp.broadcast_to(gain_ref[...], (PAD, gain_ref.shape[1]))
+
+
+def block_codes(ids_ref, turned, block_rows):
+    turned[...] = ids_ref[...].astype(jnp.float32).T
+    first = pl.multiple_of(lax.axis_index("ty") * block_rows, block_rows)
+    return turned[pl.ds(first, block_rows), :]
 
 
 def gained_rows(blocks, rows, scaled_ref):
@@ -161,23 +179,41 @@
 
 
 def qkv_kernel(
-    full_width, entry_ref, weight_hbm, out_ref, weight, gathered, scaled, sums_out, sums_in,
-    rows_out, rows_in, weight_sem, g_send, g_recv, s_send, s_recv, r_send, r_recv,
+    full_width, hidden_ref, gain_ref, ids_ref, weight_hbm, table_hbm, out_ref, words_ref,
+    weight, table, turned, gathered, scaled, sums_out, sums_in, rows_out, rows_in, words_out,
+    words_in, fetch_sem, g_send, g_recv, s_send, s_recv, r_send, r_recv, w_send, w_recv,
 ):
     me_tx, me_ty = lax.axis_index("tx"), lax.axis_index("ty")
     count_tx, count_ty = lax.axis_size("tx"), lax.axis_size("ty")
     rows = scaled.shape[0]
     columns = weight.shape[1]
-    fetch = pltpu.make_async_copy(weight_hbm, weight, weight_sem)
+    block_rows = rows // count_ty
+    entries = table.shape[1]
+    width = table.shape[2] // count_tx
+    fetch = pltpu.make_async_copy(weight_hbm, weight, fetch_sem.at[0])
     fetch.start()
-    gathered[me_tx] = entry_ref[...]
+    fetch_table = pltpu.make_async_copy(table_hbm, table, fetch_sem.at[1])
+    fetch_table.start()
+    gathered[me_tx, :rows, :] = hidden_ref[...]
+    gathered[me_tx, rows:, :] = spread_gain(gain_ref)
     greet(("tx", "ty"))
     spread_own(gathered, g_send, g_recv, "tx")
+    codes = block_codes(ids_ref, turned, block_rows)
+    entry = lax.broadcasted_iota(jnp.int32, (block_rows, entries), 1) + me_tx * entries
+    fetch_table.wait()
+    for k in range(STEPS - 1):
+        found = (codes[:, k : k + 1].astype(jnp.int32) == entry).astype(jnp.float32)
+        found = found.astype(jnp.bfloat16)
+        for d in range(count_tx):
+            words_out[d, k] = jnp.dot(
+                found, table[k, :, d * width : (d + 1) * width], preferred_element_type=jnp.float32
+            ).astype(jnp.bfloat16)
     take_all(gathered, g_send, g_recv, "tx")
+    deal(words_out, words_in, w_send, w_recv, "tx")
+    words_in[me_tx] = words_out[me_tx]
     square = gained_rows(gathered, rows, scaled)
     fetch.wait()
     tile = 512
-    block_rows = rows // count_ty
     for start in range(0, columns, tile):
         part = jnp.dot(
             scaled[...], weight[:, start : start + tile], preferred_element_type=jnp.float32
@@ -209,51 +245,66 @@
     rows_in[me_tx] = rows_out[me_tx]
     take_all(rows_in, r_send, r_recv, "tx")
     out_ref[...] = rows_in[...]
+    take_all(words_in, w_send, w_recv, "tx")
+    for k in range(STEPS - 1):
+        word = words_in[0, k].astype(jnp.float32)
+        for src in range(1, count_tx):
+            word = word + words_in[src, k].astype(jnp.float32)
+        words_ref[k] = word
     settle(gathered, g_send, g_recv, "tx")
+    settle(words_in, w_send, w_recv, "tx")
     settle(sums_in, s_send, s_recv, "ty")
     settle(rows_in, r_send, r_recv, "tx")
 
 
-def qkv_rows(entry, qkv_weight, rows, full_width, count_tx, count_ty):
+def qkv_rows(hidden, gain, ids, qkv_weight, table, full_width, count_tx, count_ty):
+    rows, part_width = hidden.shape
     columns = qkv_weight.shape[1]
     block_rows = rows // count_ty
     piece = columns // count_tx
+    width = table.shape[2] // count_tx
     dma = pltpu.SemaphoreType.DMA
+    bf16, f32 = jnp.bfloat16, jnp.float32
+    inside = pl.BlockSpec(memory_space=pltpu.VMEM)
+    outside = pl.BlockSpec(memory_space=pl.ANY)
+    by_tx, by_ty = dma((count_tx,)), dma((count_ty,))
     return pl.pallas_call(
         functools.partial(qkv_kernel, full_width),
-        out_shape=jax.ShapeDtypeStruct((count_tx, block_rows, piece), jnp.bfloat16),
-        in_specs=[
-            pl.BlockSpec(memory_space=pltpu.VMEM),
-            pl.BlockSpec(memory_space=pl.ANY),
-        ],
-        out_specs=pl.BlockSpec(memory_space=pltpu.VMEM),
+        out_shape=(
+            jax.ShapeDtypeStruct((count_tx, block_rows, piece), bf16),
+            jax.ShapeDtypeStruct((STEPS - 1, block_rows, width), f32),
+        ),
+        in_specs=[inside, inside, inside, outside, outside],
+        out_specs=(inside, inside),
         scratch_shapes=[
-            pltpu.VMEM(qkv_weight.shape, jnp.bfloat16),
-            pltpu.VMEM((count_tx,) + entry.shape, jnp.bfloat16),
-            pltpu.VMEM((rows, count_tx * entry.shape[1]), jnp.bfloat16),
-            pltpu.VMEM((count_ty, block_rows, columns + LANES), jnp.bfloat16),
-            pltpu.VMEM((count_ty, block_rows, columns + LANES), jnp.bfloat16),
-            pltpu.VMEM((count_tx, block_rows, piece), jnp.bfloat16),
-            pltpu.VMEM((count_tx, block_rows, piece), jnp.bfloat16),
-            dma,
-            dma((count_tx,)), dma((count_tx,)),
-            dma((count_ty,)), dma((count_ty,)),
-            dma((count_tx,)), dma((count_tx,)),
+            pltpu.VMEM(qkv_weight.shape, bf16),
+            pltpu.VMEM(table.shape, bf16),
+            pltpu.VMEM((rows, STEPS), f32),
+            pltpu.VMEM((count_tx, rows + PAD, part_width), bf16),
+            pltpu.VMEM((rows, count_tx * part_width), bf16),
+            pltpu.VMEM((count_ty, block_rows, columns + LANES), bf16),
+            pltpu.VMEM((count_ty, block_rows, columns + LANES), bf16),
+            pltpu.VMEM((count_tx, block_rows, piece), bf16),
+            pltpu.VMEM((count_tx, block_rows, piece), bf16),
+            pltpu.VMEM((count_tx, STEPS - 1, block_rows, width), bf16),
+            pltpu.VMEM((count_tx, STEPS - 1, block_rows, width), bf16),
+            dma((2,)),
+            by_tx, by_tx, by_ty, by_ty, by_tx, by_tx, by_tx, by_tx,
         ],
         compiler_params=pltpu.CompilerParams(
             collective_id=1, has_side_effects=True, vmem_limit_bytes=VMEM_BYTES
         ),
-    )(entry, qkv_weight)
+    )(hidden, gain, ids, qkv_weight, table)
 
 
 def tail_kernel(
-    full_width, att_ref, out_hbm, resid_ref, gain_ref, in_hbm, codes_ref, gains_ref, gate_hbm,
-    up_hbm, down_hbm, table_hbm, hidden_ref, out_ref,
+    full_width, att_ref, out_hbm, resid_ref, gain_ref, in_hbm, ids_ref, owners_ref,
+    pre_ref, head_ref, words_ref, gate_hbm, up_hbm, down_hbm, table_hbm, hidden_ref, out_ref,
     out_w, in_w, gate, up, down, table, pieces, blocks, part_out, part_in, gathered, scaled,
-    starts_out, starts_in, state, gate_sum, up_sum, pre, out, sums_out, sums_in, words_out,
-    words_in, ends, finals,
+    starts_out, starts_in, state, gate_sum, up_sum, pre, out, sums_out, sums_in, turned,
+    ends, finals,
     w_sem, a_send, a_recv, b_send, b_recv, p_send, p_recv, g_send, g_recv, s_send, s_recv,
-    pre_s, pre_r, out_s, out_r, sum_s, sum_r, word_s, word_r, end_s, end_r, fin_s, fin_r,
+    pre_s, pre_r, out_s, out_r, sum_s, sum_r, end_s, end_r, fin_s, fin_r,
 ):
     me, me_ty = lax.axis_index("tx"), lax.axis_index("ty")
     count, count_ty = lax.axis_size("tx"), lax.axis_size("ty")
@@ -261,38 +312,29 @@
     block_rows, width = state.shape
     entries = table.shape[1]
     full = width * count
-    fetch_out, fetch_table, fetch_in, *fetch_rest = [
+    fetch_out, fetch_in, *fetch_rest = [
         pltpu.make_async_copy(far, near, w_sem.at[i])
         for i, (far, near) in enumerate(
             (
                 (out_hbm, out_w),
-                (table_hbm, table),
                 (in_hbm, in_w),
                 (gate_hbm, gate),
                 (up_hbm, up),
                 (down_hbm, down),
+                (table_hbm, table),
             )
         )
     ]
-    for fetch in [fetch_out, fetch_table, fetch_in] + fetch_rest:
+    for fetch in [fetch_out, fetch_in] + fetch_rest:
         fetch.start()
     lane = lax.broadcasted_iota(jnp.int32, (block_rows, LANES), 1)
     entry = lax.broadcasted_iota(jnp.int32, (block_rows, entries), 1)
-    codes = codes_ref[me_ty]
+    codes = block_codes(ids_ref, turned, block_rows).astype(jnp.int32)
     code_lane = lax.broadcasted_iota(jnp.int32, codes.shape, 1)
 
     def chosen(k):
         code = jnp.sum(jnp.where(code_lane == k, codes, 0), axis=1, keepdims=True)
         return code - me * entries == entry
-
-    def send_words(k):
-        found = chosen(k).astype(jnp.float32).astype(jnp.bfloat16)
-        for d in range(count):
-            words_out[k, d] = jnp.dot(
-                found, table[k, :, d * width : (d + 1) * width], preferred_element_type=jnp.float32
-            ).astype(jnp.bfloat16)
-        deal(words_out.at[k], words_in.at[k], word_s.at[k], word_r.at[k], "tx")
-        words_in[k, me] = words_out[k, me]
 
     pieces[me] = att_ref[me]
     greet(("tx", "ty"))
@@ -309,13 +351,6 @@
             axis=0,
         ).astype(jnp.bfloat16)
     spread_own(blocks, b_send, b_recv, "ty")
-    fetch_table.wait()
-
-    def early_words(k, carry):
-        send_words(k)
-        return carry
-
-    lax.fori_loop(0, EARLY, early_words, 0)
     take_all(blocks, b_send, b_recv, "ty")
     fetch_out.wait()
     attended = blocks[...].reshape(rows, blocks.shape[2])
@@ -334,7 +369,7 @@
     hidden = total.astype(jnp.bfloat16)
     hidden_ref[...] = hidden
     gathered[me, :rows, :] = hidden
-    gathered[me, rows:, :] = gain_ref[...]
+    gathered[me, rows:, :] = spread_gain(gain_ref)
     spread_own(gathered, g_send, g_recv, "tx")
     take_all(gathered, g_send, g_recv, "tx")
     square = gained_rows(gathered, rows, scaled)
@@ -360,10 +395,12 @@
         buffer[k, me] = values.astype(jnp.bfloat16)
         spread_own(buffer.at[k], send_sems.at[k], recv_sems.at[k], "tx")
 
-    def gained(buffer, k, src, which):
+    def gained(buffer, k, src, factor_ref):
         values = buffer[k, src].astype(jnp.float32)
         square = jnp.sum(values * values, axis=1, keepdims=True)
-        return (values * gains_ref[which, src]).astype(jnp.bfloat16), square
+        columns = pl.ds(pl.multiple_of(src * width, width), width)
+        factor = factor_ref[:, columns].astype(jnp.float32)
+        return (values * factor).astype(jnp.bfloat16), square
 
     def score(k):
         logits = jnp.zeros((block_rows, entries), jnp.float32)
@@ -371,9 +408,9 @@
         for step in range(count):
             if step:
                 take(out.at[k], out_s.at[k], out_r.at[k], "tx", step)
-            src = lax.rem(me + count - step, count)
+            src = partner("tx", step)
             columns = pl.ds(pl.multiple_of(src * width, width), width)
-            block, term = gained(out, k, src, 1)
+            block, term = gained(out, k, src, head_ref)
             logits = logits + lax.dot_general(
                 block,
                 table[k, :, columns],
@@ -388,17 +425,13 @@
         ends[me, 1] = jnp.where(lane == k, picked, ends[me, 1])
 
     def one_step(k, carry):
-        @pl.when(k < STEPS - 1 - EARLY)
-        def _():
-            send_words(k + EARLY)
-
         square = jnp.zeros((block_rows, 1), jnp.float32)
         for step in range(count):
             if step:
                 take(pre.at[k], pre_s.at[k], pre_r.at[k], "tx", step)
-            src = lax.rem(me + count - step, count)
+            src = partner("tx", step)
             depth = pl.ds(pl.multiple_of(src * width, width), width)
-            block, term = gained(pre, k, src, 0)
+            block, term = gained(pre, k, src, pre_ref)
             gate_part = jnp.dot(block, gate[depth, :], preferred_element_type=jnp.float32)
             up_part = jnp.dot(block, up[depth, :], preferred_element_type=jnp.float32)
             if step:
@@ -411,7 +444,7 @@
         gate_part = gate_sum[...] * scale
         act = (gate_part / (1.0 + jnp.exp(-gate_part)) * (up_sum[...] * scale)).astype(jnp.bfloat16)
         for step in range(count - 1, -1, -1):
-            peer = lax.rem(me + step, count)
+            peer = partner("tx", step)
             columns = pl.ds(pl.multiple_of(peer * width, width), width)
             part = jnp.dot(act, down[:, columns], preferred_element_type=jnp.float32)
             if step:
@@ -426,6 +459,9 @@
         @pl.when(k > 0)
         def _():
             score(k - 1)
+            settle(pre.at[k - 1], pre_s.at[k - 1], pre_r.at[k - 1], "tx")
+            settle(out.at[k - 1], out_s.at[k - 1], out_r.at[k - 1], "tx")
+            settle(sums_in.at[k - 1], sum_s.at[k - 1], sum_r.at[k - 1], "tx")
 
         total = jnp.zeros((block_rows, width), jnp.float32)
         for step in range(1, count):
@@ -435,11 +471,7 @@
 
         @pl.when(k < STEPS - 1)
         def _():
-            word = words_in[k, me].astype(jnp.float32)
-            for step in range(1, count):
-                src = take(words_in.at[k], word_s.at[k], word_r.at[k], "tx", step)
-                word = word + words_in[k, src].astype(jnp.float32)
-            entering = settled + embed_gain * word
+            entering = settled + embed_gain * words_ref[k]
             state[...] = entering
             announce(pre, k + 1, entering, pre_s, pre_r)
 
@@ -459,32 +491,43 @@
     finals[me_ty] = picked - jnp.log(jnp.where(lane < STEPS, total, 1.0))
     spread_own(finals, fin_s, fin_r, "ty")
     take_all(finals, fin_s, fin_r, "ty")
-    out_ref[...] = finals[...]
+    owner = owners_ref[...]
+    mine = owner == me_ty
+    above = lax.broadcasted_iota(jnp.int32, (rows, rows), 0)
+    below = lax.broadcasted_iota(jnp.int32, (rows, rows), 1)
+    ahead = (above < below) & (above // block_rows == below // block_rows)
+    rank = jnp.dot(
+        mine.astype(jnp.float32).astype(jnp.bfloat16),
+        ahead.astype(jnp.float32).astype(jnp.bfloat16),
+        preferred_element_type=jnp.float32,
+    ).astype(jnp.int32)
+    slots = out_ref.shape[2]
+    row = lax.broadcasted_iota(jnp.int32, (1, rows), 1)
+    place = jnp.where(mine, row // block_rows * (slots // count_ty) + rank, -1)
+    select = lax.broadcasted_iota(jnp.int32, (slots, rows), 0) == place
+    placed = jnp.dot(
+        select.astype(jnp.float32),
+        finals[...].reshape(rows, LANES),
+        precision=lax.Precision.HIGHEST,
+        preferred_element_type=jnp.float32,
+    )
+    out_ref[0] = placed.T[:STEPS]
     settle(pieces, a_send, a_recv, "tx")
     settle(blocks, b_send, b_recv, "ty")
     settle(part_in, p_send, p_recv, "tx")
     settle(gathered, g_send, g_recv, "tx")
     settle(starts_in, s_send, s_recv, "ty")
 
-    def close(k, carry):
-        settle(pre.at[k], pre_s.at[k], pre_r.at[k], "tx")
-        settle(out.at[k], out_s.at[k], out_r.at[k], "tx")
-        settle(sums_in.at[k], sum_s.at[k], sum_r.at[k], "tx")
-
-        @pl.when(k < STEPS - 1)
-        def _():
-            settle(words_in.at[k], word_s.at[k], word_r.at[k], "tx")
-
-        return carry
-
-    lax.fori_loop(0, STEPS, close, 0)
+    settle(out.at[STEPS - 1], out_s.at[STEPS - 1], out_r.at[STEPS - 1], "tx")
+    settle(pre.at[STEPS - 1], pre_s.at[STEPS - 1], pre_r.at[STEPS - 1], "tx")
+    settle(sums_in.at[STEPS - 1], sum_s.at[STEPS - 1], sum_r.at[STEPS - 1], "tx")
     settle(ends, end_s, end_r, "tx")
     settle(finals, fin_s, fin_r, "ty")
 
 
 def tail_rows(
-    attended, out_weight, residual, gain, in_weight, codes, gains, mlp_gate, mlp_up, mlp_down,
-    table, full_width, count_tx, count_ty,
+    attended, out_weight, residual, gain, in_weight, ids, owners, pre_gain, head_gain, words,
+    mlp_gate, mlp_up, mlp_down, table, slots, full_width, count_tx, count_ty,
 ):
     rows, width = residual.shape
     block_rows = attended.shape[1]
@@ -500,9 +543,9 @@
         functools.partial(tail_kernel, full_width),
         out_shape=(
             jax.ShapeDtypeStruct((rows, width), bf16),
-            jax.ShapeDtypeStruct((count_ty, block_rows, LANES), f32),
+            jax.ShapeDtypeStruct((1, STEPS, slots), f32),
         ),
-        in_specs=[inside, outside, inside, inside, outside, inside, inside] + [outside] * 4,
+        in_specs=[inside, outside, inside, inside, outside] + [inside] * 5 + [outside] * 4,
         out_specs=(inside, inside),
         scratch_shapes=[
             pltpu.VMEM(out_weight.shape, bf16),
@@ -523,26 +566,23 @@
             pltpu.VMEM((block_rows, hidden_units), f32),
             pltpu.VMEM((block_rows, hidden_units), f32),
         ]
-        + [pltpu.VMEM(each + (block_rows, columns), bf16)] * 6
+        + [pltpu.VMEM(each + (block_rows, columns), bf16)] * 4
         + [
+            pltpu.VMEM((rows, STEPS), f32),
             pltpu.VMEM((count_tx, 2, block_rows, LANES), f32),
             pltpu.VMEM((count_ty, block_rows, LANES), f32),
             dma((6,)),
             by_tx, by_tx, by_ty, by_ty, by_tx, by_tx, by_tx, by_tx, by_ty, by_ty,
         ]
-        + [dma(each)] * 8
+        + [dma(each)] * 6
         + [by_tx, by_tx, by_ty, by_ty],
         compiler_params=pltpu.CompilerParams(
             collective_id=2, has_side_effects=True, vmem_limit_bytes=VMEM_BYTES
         ),
     )(
-        attended, out_weight, residual, gain, in_weight, codes, gains, mlp_gate, mlp_up, mlp_down,
-        table,
-    )
-
-
-def padded_gain(gain):
-    return jnp.pad(gain[None, :], ((0, PAD - 1), (0, 0)))
+        attended, out_weight, residual, gain, in_weight, ids, owners, pre_gain, head_gain, words,
+        mlp_gate, mlp_up, mlp_down, table,
+    )
 
 
 def body(
@@ -567,12 +607,12 @@
 ):
     count_tx = lax.axis_size("tx")
     count_ty = lax.axis_size("ty")
-    batch_rows = hidden_in.shape[0]
     own_rows = key_cache.shape[0]
-    block_rows = batch_rows // count_ty
     full_width = hidden_in.shape[1] * count_tx * count_ty
-    entry = jnp.concatenate([hidden_in, padded_gain(norm_gain)], axis=0)
-    raw = qkv_rows(entry, qkv_weight, batch_rows, full_width, count_tx, count_ty)
+    ids = codebook_ids.T
+    raw, words = qkv_rows(
+        hidden_in, norm_gain[None], ids, qkv_weight, codebook_table, full_width, count_tx, count_ty
+    )
     qkv_raw = (
         raw.reshape(count_tx, count_tx, own_rows, raw.shape[2])
         .transpose(2, 0, 1, 3)
@@ -595,35 +635,27 @@
         .transpose(1, 2, 0, 3)
         .reshape(count_tx, count_tx * own_rows, -1)
     )
-    width = in_weight.shape[1]
-    gains = jnp.stack([pre_gain, head_gain]).astype(jnp.float32)
-    hidden_out, logprob = tail_rows(
+    capacity = max(2, 2 * own_rows * count_tx // count_ty)
+    return tail_rows(
         attended,
         out_weight,
         hidden_in,
-        padded_gain(final_gain),
+        final_gain[None],
         in_weight,
-        codebook_ids.reshape(count_ty, block_rows, STEPS),
-        gains.reshape(2, count_tx, 1, width),
+        ids,
+        owners[None],
+        pre_gain[None],
+        head_gain[None],
+        words,
         mlp_gate,
         mlp_up,
         mlp_down,
         codebook_table,
+        count_ty * capacity,
         full_width,
         count_tx,
         count_ty,
     )
-    capacity = max(2, 2 * own_rows * count_tx // count_ty)
-    slot_count = count_ty * capacity
-    earlier = jnp.arange(block_rows)[:, None] > jnp.arange(block_rows)[None, :]
-    same = owners.reshape(count_ty, block_rows, 1) == owners.reshape(count_ty, 1, block_rows)
-    rank = jnp.sum((same & earlier[None]).astype(jnp.int32), axis=2)
-    slot = (jnp.arange(count_ty, dtype=jnp.int32)[:, None] * capacity + rank).reshape(-1)
-    place = jnp.where(owners == lax.axis_index("ty"), slot, -1)
-    mine = place[None, :] == jnp.arange(slot_count, dtype=jnp.int32)[:, None]
-    logprob = logprob.reshape(batch_rows, LANES)[:, :STEPS].T
-    placed_rows = jnp.sum(jnp.where(mine[None], logprob[:, None, :], 0.0), axis=2)
-    return (hidden_out, placed_rows[None])
 
 
 def solution(mesh):

time: 168 us -> 157 us (0.935)
  Pallas kernels: 149 us -> 142 us
  other arithmetic: 6.65 us -> 2.78 us
    pallas_call x1, Pallas kernels: 122 us -> 114 us  [tail_rows(): pl.pallas_call(functools.partial(tail_kernel, full_width), out_shape=(jax...]
    broadcast_in_dim x2 -> x4, local copies, waits for them, and re-layouts: 1.32 us -> 5.05 us  [the longest x1 1.3 us: body(): pre_gain[None]]
where the time goes in v3:
time: 157 us
  Pallas kernels  142 us (90%)
  local copies, waits for them, and re-layouts  9.5 us (6%)
  other arithmetic  2.78 us (2%)
    pallas_call x1, Pallas kernels, tail_rows(): pl.pallas_call(functools.partial(tail_kernel, full_width), out_shape=(jax...  114 us
    pallas_call x1, Pallas kernels, qkv_rows(): pl.pallas_call(functools.partial(qkv_kernel, full_width), out_shape=(jax....  28.4 us

profile of v3, /device:TPU:0, one launch (start us, length us, event | category | flops | bytes accessed | tf_op | source)
XLA Modules:
  0.0 156.6 jit_solution(18199369861238320103)
XLA Ops:
  0.6 0.0 copy-start
  0.6 0.7 convert_element_type.61
  1.4 0.7 iota_compare_fusion
  2.1 1.2 broadcast_in_dim.23.gain_ref
  3.4 1.2 broadcast_in_dim.41.gain_ref
  4.6 0.1 multiply_cosine_fusion
  4.7 1.3 broadcast_in_dim.43.pre_ref
  6.0 1.3 broadcast_in_dim.44.head_ref
  7.3 0.7 convert_element_type.60
  8.0 28.4 %shard_map.185 = (bf16[4,16,640]{2,1,0:T(8,128)(2,1)}, f32[7,16,512]{2,1,0:T(8,128)}) custom-call(bf16[128,256]{1,0:T(8,128)(2,1)} %resid_ref.1, bf16[1,256]{1,0:T(2,128)(2,1)} %broadcast_in_dim.23.gain_ref, s32[8,128]{1,0:T(8,128)} %bitcast.55, bf16[1024,2560]{1,0:T(8,128)(2,1)} %weight_hbm.1, bf16[8,256,2048]{2,1,0:T(8,128)(2,1)} %table_hbm.3), custom_call_target="tpu_custom_call" | custom-call | tf_op jit(solution)/shard_map/pallas_call | solution.py:271
  36.4 0.9 reshape.128
  37.5 0.1 subtract_convert_fusion
  37.6 0.1 maximum_bitcast_fusion
  37.6 0.1 subtract_bitcast_fusion
  37.7 0.1 fusion.6
  37.9 0.1 fusion.8
  38.0 0.0 copy-done
  38.0 0.7 fusion.11
  38.8 0.4 fusion.1
  39.3 0.1 copy.47
  39.3 0.6 reshape.125.att_ref
  40.0 113.8 %shard_map.186 = (bf16[128,256]{1,0:T(8,128)(2,1)}, f32[1,8,32]{2,1,0:T(8,128)}) custom-call(bf16[4,16,512]{2,1,0:T(8,128)(2,1)} %reshape.125.att_ref, bf16[2048,1024]{1,0:T(8,128)(2,1)} %out_hbm.1, bf16[128,256]{1,0:T(8,128)(2,1)} %resid_ref.1, bf16[1,256]{1,0:T(2,128)(2,1)} %broadcast_in_dim.41.gain_ref, bf16[1024,512]{1,0:T(8,128)(2,1)} %in_hbm.1, ...), custom_call_target="tpu_custom_call" | custom-call | tf_op jit(solution)/shard_map/pallas_call | solution.py:542
  153.8 1.5 copy.52
  155.3 1.3 copy.53
  (12 shorter events, 0.2 us)
Async XLA Ops:
  0.6 37.4 %copy-start = (bf16[4,128,1024]{2,1,0:T(8,128)(2,1)S(1)}, bf16[4,128,1024]{2,1,0:T(8,128)(2,1)}, u32[]{:S(2)}) copy-start(bf16[4,128,1024]{2,1,0:T(8,128)(2,1)} %param.22) | copy-start | bytes 3145732
  8.0 30.8 %copy-start.1 = (bf16[4,128,1024]{2,1,0:T(8,128)(2,1)S(1)}, bf16[4,128,1024]{2,1,0:T(8,128)(2,1)}, u32[]{:S(2)}) copy-start(bf16[4,128,1024]{2,1,0:T(8,128)(2,1)} %param.23) | copy-start | bytes 3145732
